TPU v7x, 32 devices: a whole 2x2x4 slice. The times are simulated.
32 devices in a mesh: lat: 4 (over y, x), lon: 8 (over z, core).
Axes of the slice: x: 2, y: 2, z: 4, core: 2. Of those that a mesh axis runs over, the one named last changes fastest.
Arguments:
- model_state: float32 [5, 4, 3584, 1024], P(None, None, 'lon', 'lat'), may hold values from -6 to 6
- diffusion: float32 [2, 1024], P(None, 'lat'), may hold values from 0.02 to 0.24
- coupling: float32 [4, 5, 5], replicated, may hold values from -2.5 to 2.5
- cutoff: int32 [256], replicated, may hold values from 1 to 896, as said below
- strip_list: int32 [256, 4], P(('lat', 'lon')), may hold values from 0 to 447, as said below
- nest_place: int32 [32, 8, 2], P(('lat', 'lon')), may hold values from 0 to 1872
Outputs:
- advanced_state: float32 [5, 4, 3584, 1024], P(None, None, 'lon', 'lat')
- nest_boundary: float32 [32, 5, 4, 2048], P(('lat', 'lon'))
Inputs may be any that keep to these rules, and one draw needn't show every extreme that they name: cutoff[b] is the number of kept wavenumbers of band row b; the values 1 and 896 both occur. `strip_list`: in the 8 rows of one device: column 0 names an owner (an index of lon) and no owner is named by more than 2 of these rows; at every index of lat some owner is named by exactly 2 rows of every device of that index. Column 1 is a longitude column within the device's block (below 448), column 2 a row offset within the block (at most 240), column 3 a length of 1 to 16; every device has a strip of length 16.
All inputs are finite; a program needn't handle non-finite values.
Results may differ from a plain program's by a relative error of at most 0.0001.
Values sent between devices are 32-bit elements; how exact they have to be, the bound alone decides.
No kernel may reach another device: no remote copies, remote signals or barrier semaphores. Data moves between devices by JAX's collectives and lax.ppermute only.
A program may use at most 384 MiB of HBM per device.

v0:
```python
import functools
import math

import jax
import jax.numpy as jnp
import numpy as np
from jax import lax
from jax.experimental import pallas as pl
from jax.experimental.pallas import tpu as pltpu
from jax.sharding import PartitionSpec as P

POLAR = 128
CAP = 2
STRIP = 16
RATIO = 11
NB = 2048
KC = 896
RANKS = (14, 5, 4, 4)
SPLIT_RANK = 14
STEP = 16
HELD = 80
EARLY_LISTS = 8
QUICK = (0, 2)
LATE = (3, 4)
SOUTH = 64
VMEM_LIMIT = 48 * 1024 * 1024
F32 = jnp.float32
BF16 = jnp.bfloat16


def ceil8(value):
    return -(-value // 8) * 8


def shift_ranks(count):
    shifts = []
    for step in range(1, count // 2 + 1):
        for shift in (step, -step):
            if shift != -count // 2:
                shifts.append((shift, RANKS[min(step, len(RANKS)) - 1]))
    return shifts


def is_second(place, step, count):
    return lax.rem(lax.div(place, math.gcd(step, count)), 2) == 1


def swaps(pairs):
    return [pair for a, b in pairs for pair in ((a, b), (b, a))]


def ring_swaps(step, count):
    if 2 * step == count:
        return [swaps([(i, i + step) for i in range(step)])]
    groups = [[], []]
    for i in range(count):
        groups[i // math.gcd(step, count) % 2].append((i, (i + step) % count))
    return [swaps(group) for group in groups]


def split_table(table):
    high = table.astype(jnp.bfloat16)
    low = (table - high.astype(np.float64)).astype(jnp.bfloat16)
    return high, low


def factored(block, rank):
    left, values, right = np.linalg.svd(block)
    root = np.sqrt(values[:rank])
    return right[:rank] * root[:, None], left[:, :rank] * root[None, :]


@functools.lru_cache(maxsize=None)
def filter_tables(count, width):
    total = count * width
    half = width // 2

    def block(size, shift):
        place = np.arange(size)
        angle = np.pi * (shift + place[:, None] - place[None, :]) / total
        with np.errstate(divide="ignore"):
            return np.where(angle == 0, 0.0, 1.0 / (np.sin(angle) * total))

    senders, receivers = [], []
    for shift, rank in shift_ranks(count):
        sender, receiver = factored(block(width, shift * width), rank)
        senders.append(np.pad(sender, ((0, ceil8(rank) - rank), (0, 0))))
        receivers.append(receiver)
    nears = []
    for part, shift in enumerate((half, -half)):
        sender, receiver = factored(block(half, shift), SPLIT_RANK)
        rows = np.concatenate([block(half, 0), sender], axis=0)
        nears.append(np.pad(rows, ((0, 16 - SPLIT_RANK), (0, 0))))
        beyond = ((half, 0), (0, 0)) if part == 0 else ((0, half), (0, 0))
        receivers.append(np.pad(receiver, beyond))
    receivers = np.concatenate(receivers, axis=1)
    receivers = np.pad(receivers, ((0, 0), (0, HELD - receivers.shape[1])))
    nears = [table for rows in nears for table in split_table(rows)]
    send_high, send_low = split_table(np.concatenate(senders, axis=0))
    far_high, far_low = split_table(receivers)
    return (
        np.concatenate(nears, axis=0),
        np.concatenate([send_high, send_low], axis=0),
        np.concatenate([far_high, far_high, far_low], axis=1),
    )


def hat_table():
    width = -(-STRIP * RATIO // POLAR) * POLAR
    point = np.arange(width)
    table = np.zeros((POLAR, CAP * width), np.float32)
    for rank in range(CAP):
        for row in range(STRIP):
            hat = np.maximum(RATIO - np.abs(point - row * RATIO), 0) * (point < STRIP * RATIO)
            table[rank * STRIP + row, rank * width : (rank + 1) * width] = hat
    return table.astype(jnp.bfloat16)


def split_value(value):
    high = value.astype(BF16)
    return high, (value - high.astype(F32)).astype(BF16)


def modulated(row, cosine, sine):
    return jnp.concatenate([row * cosine[...], row * sine[...]], axis=1)


def stacked(value):
    high, low = split_value(value)
    return jnp.concatenate([high, low, high], axis=0)


def strip_rows(slots):
    return slots // 2


def payload_rows(rank, slots):
    return ceil8(slots * rank + strip_rows(slots))


def edge_kernel(
    meta, state, lon_pair, lon_cross, lat_pair, lat_cross, held, edges, in_sems
):
    fields, levels, columns, rows = state.shape
    lists = fields * levels

    def copy_in(item):
        l, f = item // fields, item % fields
        return pltpu.make_async_copy(state.at[f, l], held.at[item], in_sems.at[item])

    def start(item, carry):
        copy_in(item).start()
        return carry

    lax.fori_loop(0, lists, start, 0)
    lane = lax.broadcasted_iota(jnp.int32, (columns, POLAR), 1)
    lon_odd = lax.rem(meta[2], 2) == 1
    lat_odd = lax.rem(meta[3], 2) == 1
    edges[...] = jnp.zeros(edges.shape, F32)

    def one(item, carry):
        copy_in(item).wait()
        first = held[item, 0:1, :]
        last = held[item, columns - 1 : columns, :]
        lon_pair[pl.ds(item, 1), :] = jnp.where(lon_odd, first, last)
        lon_cross[pl.ds(item, 1), :] = jnp.where(lon_odd, last, first)
        north = pltpu.roll(held[item, :, 0:POLAR], item, 1)
        south = pltpu.roll(held[item, :, rows - POLAR :], item + SOUTH + 1, 1)
        value = jnp.where(lane == item, north, edges[...])
        edges[...] = jnp.where(lane == SOUTH + item, south, value)
        return carry

    lax.fori_loop(0, lists, one, 0, unroll=5)
    turned = edges[...].T
    size = lat_pair.shape[0]
    north, south = turned[0:size], turned[SOUTH : SOUTH + size]
    lat_pair[...] = jnp.where(lat_odd, north, south)
    lat_cross[...] = jnp.where(lat_odd, south, north)


def stencil_kernel(
    count,
    meta,
    coupling,
    strips,
    lon_pair,
    lon_cross,
    lat_pair,
    lat_cross,
    diffusion,
    cosine,
    sine,
    send,
    state,
    updated,
    own,
    *rest,
):
    ranks = shift_ranks(count)
    payloads = rest[: len(ranks)]
    held, made, halos, halo, factors, placed, rows_cut, in_sems, out_sems = rest[len(ranks) :]
    fields, levels, columns, rows = state.shape
    tiles = rows // POLAR
    spans = [slice(tile * POLAR, (tile + 1) * POLAR) for tile in range(tiles)]

    def copy_in(l, f):
        return pltpu.make_async_copy(
            state.at[f, l], held.at[l, f, pl.ds(8, columns)], in_sems.at[l, f]
        )

    def copy_out(l, f):
        return pltpu.make_async_copy(made.at[l, f], updated.at[f, l], out_sems.at[l, f])

    for l in range(levels):
        for f in range(fields):
            copy_in(l, f).start()

    lane = lax.broadcasted_iota(jnp.int32, (STEP, POLAR), 1)
    lowest, highest = lane == 0, lane == POLAR - 1
    along = [jnp.broadcast_to(diffusion[0:1, span], (STEP, POLAR)) for span in spans]
    across = [jnp.broadcast_to(diffusion[1:2, span], (STEP, POLAR)) for span in spans]
    centre = [1.0 - 2.0 * along[t] - 2.0 * across[t] for t in range(tiles)]
    lon_odd = lax.rem(meta[2], 2) == 1
    lat_odd = lax.rem(meta[3], 2) == 1
    half = send.shape[0] // 2
    start = pl.multiple_of(meta[0] * POLAR, POLAR)
    size = lat_pair.shape[0]
    blank = jnp.zeros((SOUTH - size, columns), F32)
    north_halo = jnp.where(lat_odd, lat_pair[...], lat_cross[...])
    south_halo = jnp.where(lat_odd, lat_cross[...], lat_pair[...])
    halos[...] = jnp.concatenate([north_halo, blank, south_halo, blank], axis=0).T

    def one_level(l, carry):
        for f in range(fields):
            copy_in(l, f).wait()
        weights = [
            [coupling[l, f * fields + g] for g in range(fields)] for f in range(fields)
        ]
        halo[...] = pltpu.roll(halos[...], lax.rem(POLAR - l * fields, POLAR), 1)
        for f in range(fields):
            item = pl.ds(l * fields + f, 1)
            pair, cross = lon_pair[item, :], lon_cross[item, :]
            held[l, f, 7:8, :] = jnp.where(lon_odd, pair, cross)
            held[l, f, columns + 8 : columns + 9, :] = jnp.where(lon_odd, cross, pair)
        for begin in range(0, columns, STEP):
            end = begin + STEP
            shifted = lambda f, t, by: held[l, f, begin + 8 + by : end + 8 + by, spans[t]]
            here = [[shifted(f, t, 0) for t in range(tiles)] for f in range(fields)]
            edges = halo[begin:end, :]
            for f in range(fields):
                down = [pltpu.roll(here[f][t], 1, 1) for t in range(tiles)]
                up = [pltpu.roll(here[f][t], POLAR - 1, 1) for t in range(tiles)]
                north_edge = [pltpu.roll(edges, POLAR - f, 1) if f else edges] + down[:-1]
                south_edge = up[1:] + [pltpu.roll(edges, POLAR - 1 - SOUTH - f, 1)]
                for t in range(tiles):
                    north = jnp.where(lowest, north_edge[t], down[t])
                    south = jnp.where(highest, south_edge[t], up[t])
                    result = (centre[t] + weights[f][f]) * here[f][t]
                    result = result + along[t] * (shifted(f, t, 1) + shifted(f, t, -1))
                    result = result + across[t] * (north + south)
                    for g in range(fields):
                        if g != f:
                            result = result + weights[f][g] * here[g][t]
                    made[l, f, begin:end, spans[t]] = result
        for f in range(fields):
            copy_out(l, f).start()
        for f in range(fields):
            row = made[l, f, :, pl.ds(start, POLAR)]
            high, low = split_value(modulated(row, cosine, sine))
            both = jnp.dot(send[...], high, preferred_element_type=F32)
            cross = jnp.dot(send[0:half, :], low, preferred_element_type=F32)
            factors[l * fields + f] = both[:half] + both[half:] + cross
        return carry

    lax.fori_loop(0, levels, one_level, 0)

    lon_index = meta[2]
    slots = strips.shape[0]
    lists = fields * levels
    each = strip_rows(lists)
    placed[...] = jnp.zeros(placed.shape, F32)
    rows_cut[...] = jnp.zeros(rows_cut.shape, F32)
    strip_lane = lax.broadcasted_iota(jnp.int32, (16, rows), 1)

    def one_slot(s):
        owner, column = strips[s, 0], strips[s, 1]
        offset, length = strips[s, 2], strips[s, 3]
        rank = jnp.int32(0)
        for other in range(s):
            rank = rank + (strips[other, 0] == owner).astype(jnp.int32)
        for l in range(levels):
            for f in range(fields):
                side, place = divmod(l * fields + f, each)
                rows_cut[s, side, place : place + 1, :] = made[l, f, pl.ds(column, 1), :]
        base = rank * STRIP
        shift = lax.rem(owner - lon_index + count, count)
        for side in range(2):
            where = side * POLAR + base
            moved = pltpu.roll(rows_cut[s, side], lax.rem(where - offset + rows, rows), 1)
            inside = (strip_lane >= where) & (strip_lane < where + length)
            placed[shift] = placed[shift] + jnp.where(inside, moved, 0.0)

    for s in range(slots):
        one_slot(s)
    own[...] = placed[0]

    place = 0
    index = 0
    while index < len(ranks):
        step, rank = ranks[index]
        padded = ceil8(rank)
        paired = 2 if 2 * step < count else 1
        second = is_second(lon_index, step, count)
        targets = payloads[index : index + paired]
        for item in range(lists):
            span = slice(item * rank, (item + 1) * rank)
            plus = factors[item, place : place + rank, :]
            if paired == 1:
                targets[0][span, :] = plus
            else:
                minus = factors[item, place + padded : place + padded + rank, :]
                targets[0][span, :] = jnp.where(second, minus, plus)
                targets[1][span, :] = jnp.where(second, plus, minus)
        plus, minus = placed[step][0:each, :], placed[count - step][0:each, :]
        targets[0][lists * rank : lists * rank + each, :] = jnp.where(second, minus, plus)
        if paired == 2:
            targets[1][lists * rank : lists * rank + each, :] = jnp.where(second, plus, minus)
        for target in targets:
            unused = target.shape[0] - lists * rank - each
            if unused:
                target[lists * rank + each :, :] = jnp.zeros((unused, rows), F32)
        place += paired * padded
        index += paired
    for l in range(levels):
        for f in range(fields):
            copy_out(l, f).wait()


def near_kernel(begin, passed, meta, cosine, sine, middle, near, rows, *rest):
    filtered, moments = rest[passed], rest[passed + 1]
    held, sems = rest[2 * passed + 2 :]
    fields = rows.shape[0]
    lists, columns, _ = filtered.shape
    half = columns // 2
    each = near.shape[0] // 4
    mine = pl.ds(pl.multiple_of(meta[0] * POLAR, POLAR), POLAR)

    def copy_in(item):
        l, f = (begin + item) // fields, (begin + item) % fields
        return pltpu.make_async_copy(rows.at[f, l, :, mine], held.at[item], sems.at[item])

    @pl.when(meta[1] == 1)
    def _():
        for item in range(lists):
            copy_in(item).start()

        def one(item, carry):
            copy_in(item).wait()
            for part in range(2):
                span = slice(part * half, (part + 1) * half)
                row = held[item, span, :]
                turn_cos, turn_sin = cosine[span, :], sine[span, :]
                value = jnp.concatenate([row * turn_cos, row * turn_sin], axis=1)
                table = near[2 * part * each : 2 * (part + 1) * each, :]
                high, low = split_value(value)
                both = jnp.dot(table, high, preferred_element_type=F32)
                cross = jnp.dot(table[:each], low, preferred_element_type=F32)
                total = both[:each] + both[each:] + cross
                filtered[item, span, :] = (
                    turn_sin * total[:half, :POLAR]
                    - turn_cos * total[:half, POLAR:]
                    + middle[0:1, :] * row
                )
                moments[item, part * 16 : (part + 1) * 16, :] = total[half:, :]
            return carry

        lax.fori_loop(0, lists, one, 0, unroll=4)


def far_kernel(count, meta, begins, cosine, sine, turn, far, hats, own, *rest):
    ranks = shift_ranks(count)
    payloads = rest[: len(ranks)]
    near_parts = (rest[len(ranks) : len(ranks) + 2], rest[len(ranks) + 2 : len(ranks) + 4])
    _, out, boundary, filtered, arrived, sums, sems = rest[len(ranks) + 4 :]
    fields, levels = out.shape[0:2]
    lists = fields * levels
    each = strip_rows(lists)
    lon_index = meta[2]
    mine = pl.ds(pl.multiple_of(meta[0] * POLAR, POLAR), POLAR)

    def copy_out(item):
        l, f = item // fields, item % fields
        return pltpu.make_async_copy(filtered.at[item], out.at[f, l, :, mine], sems.at[item])

    def received(index, span):
        step = abs(ranks[index][0])
        if 2 * step == count:
            return payloads[index][span, :]
        base = index - index % 2
        first, last = payloads[base][span, :], payloads[base + 1][span, :]
        takes_first = is_second(lon_index, step, count)
        if index != base:
            takes_first = jnp.logical_not(takes_first)
        return jnp.where(takes_first, first, last)

    @pl.when(meta[1] == 1)
    def _():
        place = 0
        for index, (_, rank) in enumerate(ranks):
            turn_cos = turn[index : index + 1, :POLAR]
            turn_sin = turn[index : index + 1, POLAR:]
            for item in range(lists):
                value = received(index, slice(item * rank, (item + 1) * rank))
                cosines, sines = value[:, :POLAR], value[:, POLAR:]
                arrived[item, place : place + rank, :POLAR] = (
                    turn_cos * cosines + turn_sin * sines
                )
                arrived[item, place : place + rank, POLAR:] = (
                    turn_cos * sines - turn_sin * cosines
                )
            place += rank
        begin = 0
        for near, moments in near_parts:
            for item in range(near.shape[0]):
                for part in range(2):
                    at = place + part * SPLIT_RANK
                    arrived[begin + item, at : at + SPLIT_RANK, :] = moments[
                        item, part * 16 : part * 16 + SPLIT_RANK, :
                    ]
            begin += near.shape[0]
        place += 2 * SPLIT_RANK
        for item in range(lists):
            arrived[item, place:, :] = jnp.zeros((HELD - place, 2 * POLAR), F32)

        begin = 0
        for near, _ in near_parts:

            def one(item, carry, near=near, begin=begin):
                at = begin + item
                total = jnp.dot(far[...], stacked(arrived[at]), preferred_element_type=F32)
                filtered[at] = (
                    near[item] + sine[...] * total[:, :POLAR] - cosine[...] * total[:, POLAR:]
                )
                copy_out(at).start()
                return carry

            lax.fori_loop(0, near.shape[0], one, 0, unroll=4)
            begin += near.shape[0]

    sums[...] = jnp.zeros(sums.shape, F32)
    pieces, sources = [], []
    blank = jnp.zeros((16 - each, POLAR), F32)
    for index in range(-1, len(ranks)):
        if index < 0:
            shift, arrival = 0, own[0:each, :]
        else:
            shift, rank = ranks[index]
            arrival = received(index, slice(lists * rank, lists * rank + each))
        sources.append(lax.rem(lon_index - shift + count, count))
        pieces += [arrival[:, :POLAR], blank, arrival[:, POLAR:], blank]
    pieces = jnp.concatenate(pieces, axis=0)
    high = pieces.astype(BF16)
    middle, low = split_value(pieces - high.astype(F32))
    points = jnp.dot(high, hats[...], preferred_element_type=F32)
    points = points + jnp.dot(middle, hats[...], preferred_element_type=F32)
    points = points + jnp.dot(low, hats[...], preferred_element_type=F32)
    width = hats.shape[1] // CAP
    beyond = jnp.zeros((32, POLAR), F32)
    for index, source in enumerate(sources):
        for rank in range(CAP):
            place = begins[source, rank]
            offset = lax.rem(place, POLAR)
            span = points[index * 32 : (index + 1) * 32, rank * width : (rank + 1) * width]
            moved = pltpu.roll(jnp.concatenate([span, beyond], axis=1), offset, 1)
            at = pl.ds(pl.multiple_of(place - offset, POLAR), width + POLAR)
            sums[:, at] = sums[:, at] + moved
    for l in range(levels):
        for f in range(fields):
            side, row = divmod(l * fields + f, each)
            row = side * 16 + row
            boundary[0, f, l : l + 1, :] = sums[row : row + 1, 0:NB] * (1.0 / RATIO)

    @pl.when(meta[1] == 1)
    def _():
        for item in range(lists):
            copy_out(item).wait()


def phase_table(kept, steps, period):
    phase = (2 * kept - 1)[None, :] * steps[:, None] % (2 * period)
    angle = phase.astype(F32) * (math.pi / period)
    return jnp.cos(angle), jnp.sin(angle)


def cost(flops, bytes_accessed):
    return pl.CostEstimate(flops=flops, bytes_accessed=bytes_accessed, transcendentals=0)


def compressed(model_state, diffusion, coupling, cutoff, strip_list, nest_place):
    lat_index = lax.axis_index("lat")
    lon_index = lax.axis_index("lon")
    lat_count = lax.axis_size("lat")
    lon_count = lax.axis_size("lon")
    fields, levels, columns, rows = model_state.shape
    lists = fields * levels
    total_columns = columns * lon_count
    ranks = shift_ranks(lon_count)
    near, send, far = [jnp.asarray(table) for table in filter_tables(lon_count, columns)]
    params = pltpu.CompilerParams(vmem_limit_bytes=VMEM_LIMIT)
    shape = lambda *sizes: jax.ShapeDtypeStruct(sizes, F32)
    whole_state = shape(*model_state.shape)

    is_south = lat_index == lat_count - 1
    is_polar = (lat_index == 0) | is_south
    part = jnp.where(is_south, rows // POLAR - 1, 0)
    meta = jnp.stack([part, is_polar.astype(jnp.int32), lon_index, lat_index]).astype(jnp.int32)
    kept = jnp.where(lat_index < lat_count // 2, cutoff[:POLAR], cutoff[POLAR:])
    cosine, sine = phase_table(kept, jnp.arange(columns, dtype=jnp.int32), total_columns)
    steps = jnp.array([abs(shift) for shift, _ in ranks], jnp.int32)
    sign = np.array([[1.0 if shift > 0 else -1.0] for shift, _ in ranks], np.float32)
    turn_cos, turn_sin = phase_table(kept, steps, lon_count)
    turn = jnp.concatenate([turn_cos, turn_sin * sign], axis=1)
    turn = jnp.pad(turn, ((0, ceil8(len(ranks)) - len(ranks)), (0, 0)))
    middle = ((2 * kept - 1).astype(F32) / total_columns)[None, :]
    hats = jnp.asarray(hat_table())

    smem = pl.BlockSpec(memory_space=pltpu.SMEM)
    vmem = pl.BlockSpec(memory_space=pltpu.VMEM)
    hbm = pl.BlockSpec(memory_space=pl.ANY)
    level_sems = pltpu.SemaphoreType.DMA((levels, fields))

    with jax.named_scope("edges"):
        edges = pl.pallas_call(
            edge_kernel,
            in_specs=[smem, hbm],
            out_specs=[vmem] * 4,
            out_shape=[shape(ceil8(lists), rows)] * 2 + [shape(ceil8(lists), columns)] * 2,
            scratch_shapes=[
                pltpu.VMEM((lists, columns, rows), F32),
                pltpu.VMEM((columns, POLAR), F32),
                pltpu.SemaphoreType.DMA((lists,)),
            ],
            compiler_params=params,
        )(meta, model_state)

    with jax.named_scope("halo"):
        lon_pairs, lon_crosses = ring_swaps(1, lon_count)
        lat_pairs = [(i, i + 1) for i in range(0, lat_count, 2)]
        lat_crosses = [(i, i + 1) for i in range(1, lat_count - 1, 2)]
        halos = [
            lax.ppermute(edges[0], "lon", lon_pairs),
            lax.ppermute(edges[1], "lon", lon_crosses),
            lax.ppermute(edges[2], "lat", swaps(lat_pairs)),
            lax.ppermute(edges[3], "lat", swaps(lat_crosses)),
        ]

    sizes = [payload_rows(rank, lists) for _, rank in ranks]
    with jax.named_scope("stencil"):
        updated, own, *outgoing = pl.pallas_call(
            functools.partial(stencil_kernel, lon_count),
            in_specs=[smem] * 3 + [vmem] * 8 + [hbm],
            out_specs=[hbm] + [vmem] * (1 + len(ranks)),
            out_shape=[whole_state, shape(16, rows)] + [shape(size, rows) for size in sizes],
            scratch_shapes=[
                pltpu.VMEM((levels, fields, columns + 16, rows), F32),
                pltpu.VMEM((levels, fields, columns, rows), F32),
                pltpu.VMEM((columns, POLAR), F32),
                pltpu.VMEM((columns, POLAR), F32),
                pltpu.VMEM((lists, send.shape[0] // 2, rows), F32),
                pltpu.VMEM((lon_count, 16, rows), F32),
                pltpu.VMEM((strip_list.shape[0], 2, 16, rows), F32),
                level_sems,
                level_sems,
            ],
            compiler_params=params,
        )(
            meta,
            coupling.reshape(levels, fields * fields),
            strip_list,
            *halos,
            diffusion,
            cosine,
            sine,
            send,
            model_state,
        )

    def exchange(index, payload):
        step = abs(ranks[index][0])
        swap = index % 2 if 2 * step < lon_count else 0
        return lax.ppermute(payload, "lon", ring_swaps(step, lon_count)[swap])

    with jax.named_scope("exchange"):
        incoming = {
            index: exchange(index, outgoing[index])
            for index in range(len(ranks))
            if index not in LATE
        }

    def near_part(begin, end, passed):
        results = pl.pallas_call(
            functools.partial(near_kernel, begin, len(passed)),
            in_specs=[smem] + [vmem] * 4 + [hbm] * (1 + len(passed)),
            out_specs=[vmem] * 2 + [hbm] * len(passed),
            out_shape=[shape(end - begin, columns, POLAR), shape(end - begin, 32, rows)]
            + [shape(*payload.shape) for payload in passed],
            input_output_aliases={6 + index: 2 + index for index in range(len(passed))},
            scratch_shapes=[
                pltpu.VMEM((end - begin, columns, POLAR), F32),
                pltpu.SemaphoreType.DMA((end - begin,)),
            ],
            compiler_params=params,
            cost_estimate=cost(
                12 * (end - begin) * columns * columns * POLAR, 8 * (end - begin) * columns * POLAR
            ),
        )(meta, cosine, sine, middle, near, updated, *passed)
        return results[:2], results[2:]

    with jax.named_scope("near"):
        near_first, passed = near_part(0, EARLY_LISTS, [outgoing[index] for index in LATE])
    with jax.named_scope("late_exchange"):
        for index, payload in zip(LATE, passed):
            incoming[index] = exchange(index, payload)
    with jax.named_scope("near_rest"):
        near_last, passed = near_part(EARLY_LISTS, lists, [incoming[index] for index in QUICK])
        incoming.update(zip(QUICK, passed))

    with jax.named_scope("far"):
        advanced, boundary = pl.pallas_call(
            functools.partial(far_kernel, lon_count),
            in_specs=[smem] * 2 + [vmem] * (10 + len(ranks)) + [hbm],
            out_specs=[hbm, vmem],
            out_shape=[whole_state, shape(1, fields, levels, NB)],
            input_output_aliases={12 + len(ranks): 0},
            scratch_shapes=[
                pltpu.VMEM((lists, columns, POLAR), F32),
                pltpu.VMEM((lists, HELD, rows), F32),
                pltpu.VMEM((32, NB + 2 * POLAR), F32),
                pltpu.SemaphoreType.DMA((lists,)),
            ],
            compiler_params=pltpu.CompilerParams(vmem_limit_bytes=VMEM_LIMIT // 2),
        )(
            meta,
            nest_place.reshape(lon_count, CAP),
            cosine,
            sine,
            turn,
            far,
            hats,
            own,
            *[incoming[index] for index in range(len(ranks))],
            *near_first,
            *near_last,
            updated,
        )
    return advanced, boundary


def padded_2(block, sides, width):
    for axis, dim in sides:
        count = lax.axis_size(axis)
        forward = [(i, i + 1) for i in range(count - 1)]
        forward.append((count - 1, 0))
        backward = [(target, source) for source, target in forward]
        low = lax.ppermute(
            lax.slice_in_dim(block, block.shape[dim] - width, None, axis=dim), axis, forward
        )
        high = lax.ppermute(lax.slice_in_dim(block, 0, width, axis=dim), axis, backward)
        block = jnp.concatenate([low, block, high], axis=dim)
    return block


def spectral_filter(rows, kept):
    top_wavenumber_kept = lax.Precision.HIGHEST
    length = rows.shape[3]
    width = math.gcd(KC, 128)
    column_grid = lax.broadcasted_iota(jnp.int32, (length, width), 0)
    step_output = jnp.zeros_like(rows)
    for block_index in range(KC // width):
        wavenumber = block_index * width + lax.broadcasted_iota(jnp.int32, (length, width), 1)
        phase = column_grid * wavenumber % length
        angle = phase.astype(jnp.float32) * (2.0 * math.pi / length)
        cosine = jnp.cos(angle)
        sine = jnp.sin(angle)
        along = block_index * width + jnp.arange(width, dtype=jnp.int32)
        scale = jnp.where(along == 0, 1.0 / length, 2.0 / length)
        weight = jnp.where(along[None, :] < kept[:, None], scale[None, :], 0.0)
        real_part = (
            jnp.einsum("flrn,nk->flrk", rows, cosine, precision=top_wavenumber_kept) * weight
        )
        imaginary_component = (
            jnp.einsum("flrn,nk->flrk", rows, sine, precision=top_wavenumber_kept) * weight
        )
        step_output = (
            step_output
            + jnp.einsum("flrk,nk->flrn", real_part, cosine, precision=top_wavenumber_kept)
            + jnp.einsum("flrk,nk->flrn", imaginary_component, sine, precision=top_wavenumber_kept)
        )
    return step_output


def polar_pass(work_rows, kept_start, kept_table):
    count = work_rows.shape[2] // lax.axis_size("lon")
    kept = lax.dynamic_slice_in_dim(kept_table, kept_start + lax.axis_index("lon") * count, count)
    return lax.all_to_all(
        spectral_filter(
            lax.all_to_all(work_rows, "lon", split_axis=2, concat_axis=3, tiled=True), kept
        ),
        "lon",
        split_axis=3,
        concat_axis=2,
        tiled=True,
    )


def transposed(model_state, diffusion, coupling, cutoff, strip_list, nest_place):
    top_wavenumber_kept = lax.Precision.HIGHEST
    lat_index = lax.axis_index("lat")
    lat_count = lax.axis_size("lat")
    lon_count = lax.axis_size("lon")
    fields, levels, lon_local, lat_local = model_state.shape
    padded = padded_2(model_state, (("lat", 3), ("lon", 2)), 1)
    east_west = padded[:, :, 2:, 1:-1] + padded[:, :, :-2, 1:-1]
    row_place = lax.broadcasted_iota(jnp.int32, (1, 1, 1, lat_local), 3)
    northern = jnp.where((lat_index == 0) & (row_place == 0), 0.0, padded[:, :, 1:-1, :-2])
    southern = jnp.where(
        (lat_index == lat_count - 1) & (row_place == lat_local - 1), 0.0, padded[:, :, 1:-1, 2:]
    )
    blended = jnp.einsum("lfg,glij->flij", coupling, model_state, precision=top_wavenumber_kept)
    updated = (
        model_state
        + diffusion[0] * (east_west - 2.0 * model_state)
        + diffusion[1] * (northern + southern - 2.0 * model_state)
        + blended
    )
    is_south = lat_index == lat_count - 1
    is_polar = (lat_index == 0) | is_south
    start = jnp.where(is_south, lat_local - POLAR, 0).astype(jnp.int32)
    band_base = jnp.where(lat_index < lat_count // 2, 0, POLAR).astype(jnp.int32)
    block_rows = lax.dynamic_slice_in_dim(updated, start, POLAR, 3)
    polar_rows = jnp.transpose(block_rows, (0, 1, 3, 2))
    filtered = polar_pass(polar_rows, band_base, cutoff)
    new_rows = jnp.where(is_polar, jnp.transpose(filtered, (0, 1, 3, 2)), block_rows)
    advanced_state = lax.dynamic_update_slice_in_dim(updated, new_rows, start, 3)
    slots = strip_list.shape[0]
    owners = strip_list[:, 0]
    columns = strip_list[:, 1]
    offsets = strip_list[:, 2]
    lengths = strip_list[:, 3]
    zero = jnp.zeros((), jnp.int32)

    def cut_strip(column, offset):
        return lax.dynamic_slice(
            updated, (zero, zero, column, offset), (fields, levels, 1, STRIP)
        ).reshape(fields * levels, STRIP)

    boundary_strips = jax.vmap(cut_strip)(columns, offsets)
    inside = lax.broadcasted_iota(jnp.int32, (1, 1, STRIP), 2) < lengths[:, None, None]
    boundary_strips = jnp.where(inside, boundary_strips, 0.0).reshape(
        slots, fields * levels * STRIP
    )
    slot_ids = jnp.arange(slots, dtype=jnp.int32)
    earlier = slot_ids[None, :] < slot_ids[:, None]
    same = owners[:, None] == owners[None, :]
    rank = jnp.sum((same & earlier).astype(jnp.int32), axis=1)
    target = owners * CAP + rank
    routing = (jnp.arange(lon_count * CAP, dtype=jnp.int32)[:, None] == target[None, :]).astype(
        jnp.float32
    )
    outgoing = jnp.dot(
        routing, boundary_strips, precision=top_wavenumber_kept, preferred_element_type=jnp.float32
    ).reshape(lon_count, CAP, fields * levels * STRIP)
    arrived = lax.all_to_all(outgoing, "lon", split_axis=0, concat_axis=0, tiled=True)
    total = lon_count * CAP
    group = math.gcd(total, 16)
    pieces = arrived.reshape(total // group, group, fields * levels, STRIP)
    starts = nest_place.reshape(total // group, group)
    point = lax.broadcasted_iota(jnp.int32, (1, 1, NB), 2)
    row_step = lax.broadcasted_iota(jnp.int32, (1, STRIP, 1), 1) * RATIO

    def accumulate(carry, item):
        piece, begin = item
        offset = point - begin[:, None, None]
        hat = jnp.maximum(RATIO - jnp.abs(offset - row_step), 0)
        hat = (
            jnp.where((offset >= 0) & (offset < STRIP * RATIO), hat, 0).astype(jnp.float32) / RATIO
        )
        return (carry + jnp.einsum("gat,gtp->ap", piece, hat, precision=top_wavenumber_kept), None)

    boundary = lax.scan(
        accumulate, jnp.zeros((fields * levels, NB), jnp.float32), (pieces, starts)
    )[0]
    return (advanced_state, boundary.reshape(1, fields, levels, NB))


def local(model_state, *others):
    columns = model_state.shape[2]
    fits = lax.axis_size("lon") * STRIP == POLAR and model_state.shape[3] == 2 * POLAR
    if fits and columns % STEP == 0 and columns >= 2 * HELD:
        return compressed(model_state, *others)
    return transposed(model_state, *others)


def solution(mesh):
    return jax.shard_map(
        local,
        mesh=mesh,
        in_specs=(
            P(None, None, "lon", "lat"),
            P(None, "lat"),
            P(),
            P(),
            P(("lat", "lon"), None),
            P(("lat", "lon"), None, None),
        ),
        out_specs=(P(None, None, "lon", "lat"), P(("lat", "lon"), None, None, None)),
        check_vma=False,
    )
```

profile of v0, /device:TPU:12, one launch (start us, length us, event | category | flops | bytes accessed | tf_op | source)
XLA Modules:
  0.0 57.0 jit_solution(1457484907771722606)
XLA Ops:
  0.6 0.0 copy-start.9
  0.6 0.0 copy-start.10
  0.7 0.0 copy-start.2
  0.7 0.1 pad_add_fusion.meta
  0.8 5.6 %edges.1 = (f32[24,256]{1,0:T(8,128)S(1)}, f32[24,256]{1,0:T(8,128)S(1)}, f32[24,448]{1,0:T(8,128)S(1)}, f32[24,448]{1,0:T(8,128)S(1)}) custom-call(s32[4]{0:T(128)S(1)} %pad_add_fusion.meta, f32[5,4,448,256]{3,2,1,0:T(8,128)} %state.3), custom_call_target="tpu_custom_call" | custom-call | tf_op jit(solution)/shard_map/edges/pallas_call | solution.py:533
  6.4 0.1 collective-permute-start
  6.5 0.6 collective-permute-start.1
  7.1 1.5 %collective-permute-start.2 = (f32[24,448]{1,0:T(8,128)S(1)}, f32[24,448]{1,0:T(8,128)S(1)}, u32[]{:S(2)}, u32[]{:S(2)}) collective-permute-start(f32[24,448]{1,0:T(8,128)S(1)} %get-tuple-element.25), channel_id=1, source_target_pairs={{0,8},{8,0},{16,24},{24,16},{1,9},{9,1},{17,25},{25,17},{2,10},{10... | collective-permute-start | bytes 129032 | tf_op jit(solution)/shard_map/halo/ppermute | solution.py:553
  8.5 2.0 %collective-permute-start.3 = (f32[24,448]{1,0:T(8,128)S(1)}, f32[24,448]{1,0:T(8,128)S(1)}, u32[]{:S(2)}, u32[]{:S(2)}) collective-permute-start(f32[24,448]{1,0:T(8,128)S(1)} %get-tuple-element.26), channel_id=1, source_target_pairs={{8,16},{16,8},{9,17},{17,9},{10,18},{18,10},{11,19},{19,11},{12,20... | collective-permute-start | bytes 129032 | tf_op jit(solution)/shard_map/halo/ppermute | solution.py:554
  10.6 1.0 %fusion.4 = (f32[448,128]{1,0:T(8,128)S(1)}, f32[448,128]{1,0:T(8,128)S(1)}) fusion(s32[128]{0:T(128)S(1)} %get-tuple-element.45), kind=kLoop, calls=%fused_computation.6 | loop fusion | flops 516096 | bytes 459264 | tf_op jit(solution)/shard_map/sin | solution.py:492
  11.5 0.1 fusion.10
  11.7 0.1 copy.23.strips
  11.8 0.1 copy.24.begins
  11.8 0.1 reshape.13.coupling
  11.9 0.0 collective-permute-done.2.lat_pair
  11.9 4.0 %collective-permute-done.3.lat_cross = f32[24,448]{1,0:T(8,128)S(1)} collective-permute-done((f32[24,448]{1,0:T(8,128)S(1)}, f32[24,448]{1,0:T(8,128)S(1)}, u32[]{:S(2)}, u32[]{:S(2)}) %collective-permute-start.3) | collective-permute-done | bytes 43040 | tf_op jit(solution)/shard_map/halo/ppermute | solution.py:554
  15.9 13.6 %stencil.1 = (f32[5,4,448,256]{3,2,1,0:T(8,128)}, f32[16,256]{1,0:T(8,128)S(1)}, f32[296,256]{1,0:T(8,128)S(1)}, f32[296,256]{1,0:T(8,128)S(1)}, f32[112,256]{1,...) custom-call(s32[4]{0:T(128)S(1)} %pad_add_fusion.meta, ...), custom_call_target="tpu_custom_call" | custom-call | tf_op jit(solution)/shard_map/stencil/pallas_call | solution.py:559
  29.5 0.1 collective-permute-start.4
  29.6 2.2 %collective-permute-start.9 = (f32[96,256]{1,0:T(8,128)S(1)}, f32[96,256]{1,0:T(8,128)S(1)}, u32[]{:S(2)}, u32[]{:S(2)}) collective-permute-start(f32[96,256]{1,0:T(8,128)S(1)} %get-tuple-element.38), channel_id=1, source_target_pairs={{1,4},{4,1},{3,6},{6,3},{5,0},{0,5},{7,2},{2,7},{9,12},{12,9},{11,... | collective-permute-start | bytes 294920 | tf_op jit(solution)/shard_map/exchange/ppermute | solution.py:591
  31.8 0.8 %collective-permute-start.10 = (f32[96,256]{1,0:T(8,128)S(1)}, f32[96,256]{1,0:T(8,128)S(1)}, u32[]{:S(2)}, u32[]{:S(2)}) collective-permute-start(f32[96,256]{1,0:T(8,128)S(1)} %get-tuple-element.39), channel_id=1, source_target_pairs={{0,4},{4,0},{1,5},{5,1},{2,6},{6,2},{3,7},{7,3},{8,12},{12,8},{9,1... | collective-permute-start | bytes 294920 | tf_op jit(solution)/shard_map/exchange/ppermute | solution.py:591
  32.6 3.1 %collective-permute-start.5 = (f32[112,256]{1,0:T(8,128)S(1)}, f32[112,256]{1,0:T(8,128)S(1)}, u32[]{:S(2)}, u32[]{:S(2)}) collective-permute-start(f32[112,256]{1,0:T(8,128)S(1)} %get-tuple-element.30), channel_id=1, source_target_pairs={{0,2},{2,0},{1,3},{3,1},{4,6},{6,4},{5,7},{7,5},{8,10},{10,8},{9,1... | collective-permute-start | bytes 344072 | tf_op jit(solution)/shard_map/exchange/ppermute | solution.py:591
  35.7 0.6 %near.3 = (f32[8,448,128]{2,1,0:T(8,128)S(1)}, f32[8,32,256]{2,1,0:T(8,128)S(1)}, f32[112,256]{1,0:T(8,128)S(1)}, f32[96,256]{1,0:T(8,128)S(1)}) custom-call(s32[4]{0:T(128)S(1)} %pad_add_fusion.meta, f32[448,128]{1,0:T(8,128)S(1)} %get-tuple-element.49.cosine, f32[448,128]{1,0:T(8,128)S(1)} %get-tuple-element.48.sine, ...), custom_call_target="tpu_custom_call", output_to_operand_aliasing={{2}: (6, {}), {3}: (7, {})} | custom-call | flops 2466250752 | bytes 3670016 | tf_op jit(solution)/shard_map/near/pallas_call | solution.py:601
  36.4 0.0 copy-start.1
  36.4 0.0 copy-start.3
  36.4 9.1 %collective-permute-done.5.rest_1_ = f32[112,256]{1,0:T(8,128)S(1)} collective-permute-done((f32[112,256]{1,0:T(8,128)S(1)}, f32[112,256]{1,0:T(8,128)S(1)}, u32[]{:S(2)}, u32[]{:S(2)}) %collective-permute-start.5) | collective-permute-done | bytes 114720 | tf_op jit(solution)/shard_map/exchange/ppermute | solution.py:591
  45.5 0.0 collective-permute-start.8
  45.5 0.0 collective-permute-done.4.rest_0_
  45.5 0.0 collective-permute-start.7
  45.5 0.7 %near_rest.1 = (f32[12,448,128]{2,1,0:T(8,128)S(1)}, f32[12,32,256]{2,1,0:T(8,128)S(1)}, f32[296,256]{1,0:T(8,128)S(1)}, f32[112,256]{1,0:T(8,128)S(1)}) custom-call(s32[4]{0:T(128)S(1)} %pad_add_fusion.meta, f32[448,128]{1,0:T(8,128)S(1)} %get-tuple-element.49.cosine, ...), custom_call_target="tpu_custom_call", output_to_operand_aliasing={{2}: (6, {}), {3}: (7, {})} | custom-call | flops 3699376128 | bytes 5505024 | tf_op jit(solution)/shard_map/near_rest/pallas_call | solution.py:601
  46.2 7.4 %collective-permute-done.8.rest_4_ = f32[96,256]{1,0:T(8,128)S(1)} collective-permute-done((f32[96,256]{1,0:T(8,128)S(1)}, f32[96,256]{1,0:T(8,128)S(1)}, u32[]{:S(2)}, u32[]{:S(2)}) %collective-permute-start.8) | collective-permute-done | bytes 98336 | tf_op jit(solution)/shard_map/late_exchange/ppermute | solution.py:591
  53.6 1.4 %collective-permute-done.7.rest_3_ = f32[112,256]{1,0:T(8,128)S(1)} collective-permute-done((f32[112,256]{1,0:T(8,128)S(1)}, f32[112,256]{1,0:T(8,128)S(1)}, u32[]{:S(2)}, u32[]{:S(2)}) %collective-permute-start.7) | collective-permute-done | bytes 114720 | tf_op jit(solution)/shard_map/late_exchange/ppermute | solution.py:591
  55.0 2.0 %far.2 = (f32[5,4,448,256]{3,2,1,0:T(8,128)}, f32[1,5,4,2048]{3,2,1,0:T(4,128)}) custom-call(s32[4]{0:T(128)S(1)} %pad_add_fusion.meta, s32[8,2]{1,0:T(8,128)S(1)} %copy.24.begins, f32[448,128]{1,0:T(8,128)S(1)} %get-tuple-element.49.cosine, f32[448,128]{1,0:T(8,128)S(1)} %get-tuple-element.48.sine, ...), custom_call_target="tpu_custom_call", output_to_operand_aliasing={{0}: (19, {})} | custom-call | tf_op jit(solution)/shard_map/far/pallas_call | solution.py:629
  (26 shorter events, 0.1 us)
Async XLA Ops:
  0.6 10.9 %copy-start.9 = (f32[7]{0:T(128)S(1)}, f32[7]{0:T(128)}, u32[]{:S(2)}) copy-start(f32[7]{0:T(128)} %constant.76) | copy-start | bytes 88
  0.6 10.9 %copy-start.10 = (s32[7]{0:T(128)S(1)}, s32[7]{0:T(128)}, u32[]{:S(2)}) copy-start(s32[7]{0:T(128)} %constant.69.clone) | copy-start | bytes 88
  0.7 15.2 %copy-start.2 = (bf16[144,448]{1,0:T(8,128)(2,1)S(1)}, bf16[144,448]{1,0:T(8,128)(2,1)}, u32[]{:S(2)}) copy-start(bf16[144,448]{1,0:T(8,128)(2,1)} %constant.67.clone.send) | copy-start | bytes 387076
  0.7 9.9 %copy-start.8 = (s32[256]{0:T(256)S(1)}, s32[256]{0:T(256)}, u32[]{:S(2)}) copy-start(s32[256]{0:T(256)} %param.15) | copy-start | bytes 3076
  0.7 11.0 %copy-start.6 = (s32[8,4]{0,1:T(4,128)S(1)}, s32[8,4]{0,1:T(4,128)}, u32[]{:S(2)}) copy-start(s32[8,4]{0,1:T(4,128)} %param.16) | copy-start | bytes 388
  0.7 11.1 %copy-start.7 = (s32[1,8,2]{1,2,0:T(2,128)S(1)}, s32[1,8,2]{1,2,0:T(2,128)}, u32[]{:S(2)}) copy-start(s32[1,8,2]{1,2,0:T(2,128)} %param.17) | copy-start | bytes 196
  0.7 11.1 %copy-start.5 = (f32[4,5,5]{2,0,1:T(4,128)S(1)}, f32[4,5,5]{2,0,1:T(4,128)}, u32[]{:S(2)}) copy-start(f32[4,5,5]{2,0,1:T(4,128)} %param.14) | copy-start | bytes 1204
  0.7 15.2 %copy-start.4 = (f32[2,256]{1,0:T(2,128)S(1)}, f32[2,256]{1,0:T(2,128)}, u32[]{:S(2)}) copy-start(f32[2,256]{1,0:T(2,128)} %diffusion.1) | copy-start | bytes 6148
  0.8 34.9 %copy-start = (bf16[960,224]{1,0:T(8,128)(2,1)S(1)}, bf16[960,224]{1,0:T(8,128)(2,1)}, u32[]{:S(2)}) copy-start(bf16[960,224]{1,0:T(8,128)(2,1)} %constant.66.clone.near) | copy-start | bytes 1290244
  6.4 5.5 %collective-permute-start = (f32[24,256]{1,0:T(8,128)S(1)}, f32[24,256]{1,0:T(8,128)S(1)}, u32[]{:S(2)}, u32[]{:S(2)}) collective-permute-start(f32[24,256]{1,0:T(8,128)S(1)} %get-tuple-element.23), channel_id=1, source_target_pairs={{0,1},{1,0},{2,3},{3,2},{4,5},{5,4},{6,7},{7,6},{8,9},{9,8},{10,11... | collective-permute-start | bytes 73736 | tf_op jit(solution)/shard_map/halo/ppermute | solution.py:551
  6.5 5.4 %collective-permute-start.1 = (f32[24,256]{1,0:T(8,128)S(1)}, f32[24,256]{1,0:T(8,128)S(1)}, u32[]{:S(2)}, u32[]{:S(2)}) collective-permute-start(f32[24,256]{1,0:T(8,128)S(1)} %get-tuple-element.24), channel_id=1, source_target_pairs={{1,2},{2,1},{3,4},{4,3},{5,6},{6,5},{7,0},{0,7},{9,10},{10,9},{11,... | collective-permute-start | bytes 73736 | tf_op jit(solution)/shard_map/halo/ppermute | solution.py:552
  7.1 4.9 %collective-permute-start.2 = (f32[24,448]{1,0:T(8,128)S(1)}, f32[24,448]{1,0:T(8,128)S(1)}, u32[]{:S(2)}, u32[]{:S(2)}) collective-permute-start(f32[24,448]{1,0:T(8,128)S(1)} %get-tuple-element.25), channel_id=1, source_target_pairs={{0,8},{8,0},{16,24},{24,16},{1,9},{9,1},{17,25},{25,17},{2,10},{10... | collective-permute-start | bytes 129032 | tf_op jit(solution)/shard_map/halo/ppermute | solution.py:553
  8.5 7.4 %collective-permute-start.3 = (f32[24,448]{1,0:T(8,128)S(1)}, f32[24,448]{1,0:T(8,128)S(1)}, u32[]{:S(2)}, u32[]{:S(2)}) collective-permute-start(f32[24,448]{1,0:T(8,128)S(1)} %get-tuple-element.26), channel_id=1, source_target_pairs={{8,16},{16,8},{9,17},{17,9},{10,18},{18,10},{11,19},{19,11},{12,20... | collective-permute-start | bytes 129032 | tf_op jit(solution)/shard_map/halo/ppermute | solution.py:554
  29.5 16.0 %collective-permute-start.4 = (f32[296,256]{1,0:T(8,128)S(1)}, f32[296,256]{1,0:T(8,128)S(1)}, u32[]{:S(2)}, u32[]{:S(2)}) collective-permute-start(f32[296,256]{1,0:T(8,128)S(1)} %get-tuple-element.29), channel_id=1, source_target_pairs={{0,1},{1,0},{2,3},{3,2},{4,5},{5,4},{6,7},{7,6},{8,9},{9,8},{10,11... | collective-permute-start | bytes 909320 | tf_op jit(solution)/shard_map/exchange/ppermute | solution.py:591
  29.6 16.5 %collective-permute-start.9 = (f32[96,256]{1,0:T(8,128)S(1)}, f32[96,256]{1,0:T(8,128)S(1)}, u32[]{:S(2)}, u32[]{:S(2)}) collective-permute-start(f32[96,256]{1,0:T(8,128)S(1)} %get-tuple-element.38), channel_id=1, source_target_pairs={{1,4},{4,1},{3,6},{6,3},{5,0},{0,5},{7,2},{2,7},{9,12},{12,9},{11,... | collective-permute-start | bytes 294920 | tf_op jit(solution)/shard_map/exchange/ppermute | solution.py:591
  31.8 14.4 %collective-permute-start.10 = (f32[96,256]{1,0:T(8,128)S(1)}, f32[96,256]{1,0:T(8,128)S(1)}, u32[]{:S(2)}, u32[]{:S(2)}) collective-permute-start(f32[96,256]{1,0:T(8,128)S(1)} %get-tuple-element.39), channel_id=1, source_target_pairs={{0,4},{4,0},{1,5},{5,1},{2,6},{6,2},{3,7},{7,3},{8,12},{12,8},{9,1... | collective-permute-start | bytes 294920 | tf_op jit(solution)/shard_map/exchange/ppermute | solution.py:591
  32.6 12.9 %collective-permute-start.5 = (f32[112,256]{1,0:T(8,128)S(1)}, f32[112,256]{1,0:T(8,128)S(1)}, u32[]{:S(2)}, u32[]{:S(2)}) collective-permute-start(f32[112,256]{1,0:T(8,128)S(1)} %get-tuple-element.30), channel_id=1, source_target_pairs={{0,2},{2,0},{1,3},{3,1},{4,6},{6,4},{5,7},{7,5},{8,10},{10,8},{9,1... | collective-permute-start | bytes 344072 | tf_op jit(solution)/shard_map/exchange/ppermute | solution.py:591
  35.7 19.3 %collective-permute-start.6 = (f32[296,256]{1,0:T(8,128)S(1)}, f32[296,256]{1,0:T(8,128)S(1)}, u32[]{:S(2)}, u32[]{:S(2)}) collective-permute-start(f32[296,256]{1,0:T(8,128)S(1)} %get-tuple-element.32), channel_id=1, source_target_pairs={{1,2},{2,1},{3,4},{4,3},{5,6},{6,5},{7,0},{0,7},{9,10},{10,9},{11,... | collective-permute-start | bytes 909320 | tf_op jit(solution)/shard_map/exchange/ppermute | solution.py:591
  36.4 18.6 %copy-start.1 = (bf16[448,240]{1,0:T(8,128)(2,1)S(1)}, bf16[448,240]{1,0:T(8,128)(2,1)}, u32[]{:S(2)}) copy-start(bf16[448,240]{1,0:T(8,128)(2,1)} %constant.68.clone.far) | copy-start | bytes 645124
  36.4 18.6 %copy-start.3 = (bf16[128,512]{1,0:T(8,128)(2,1)S(1)}, bf16[128,512]{1,0:T(8,128)(2,1)}, u32[]{:S(2)}) copy-start(bf16[128,512]{1,0:T(8,128)(2,1)} %constant.71.clone.hats) | copy-start | bytes 393220
  45.5 8.1 %collective-permute-start.8 = (f32[96,256]{1,0:T(8,128)S(1)}, f32[96,256]{1,0:T(8,128)S(1)}, u32[]{:S(2)}, u32[]{:S(2)}) collective-permute-start(f32[96,256]{1,0:T(8,128)S(1)} %get-tuple-element.37), channel_id=1, source_target_pairs={{0,3},{3,0},{2,5},{5,2},{4,7},{7,4},{6,1},{1,6},{8,11},{11,8},{10,... | collective-permute-start | bytes 294920 | tf_op jit(solution)/shard_map/late_exchange/ppermute | solution.py:591
  45.5 9.5 %collective-permute-start.7 = (f32[112,256]{1,0:T(8,128)S(1)}, f32[112,256]{1,0:T(8,128)S(1)}, u32[]{:S(2)}, u32[]{:S(2)}) collective-permute-start(f32[112,256]{1,0:T(8,128)S(1)} %get-tuple-element.36), channel_id=1, source_target_pairs={{2,4},{4,2},{3,5},{5,3},{6,0},{0,6},{7,1},{1,7},{10,12},{12,10},{1... | collective-permute-start | bytes 344072 | tf_op jit(solution)/shard_map/late_exchange/ppermute | solution.py:591
where the time goes:
time: 57.7 us; the launch traced here: 57 us
  Pallas kernels  22.5 us (39%)
  waiting for transfers between devices  21.9 us (38%)
  starting transfers between devices  10.3 us (18%)
  other arithmetic  1.18 us (2%)
  between operations  0.86 us (1%)
    ppermute x7, waiting for transfers between devices, exchange(): return lax.ppermute(payload, 'lon', ring_swaps(step, lon_count)[swap])  17.9 us
    pallas_call x1, Pallas kernels, compressed(): pl.pallas_call(functools.partial(stencil_kernel, lon_count), in_specs=[sm...  13.6 us
    ppermute x7, starting transfers between devices, exchange(): return lax.ppermute(payload, 'lon', ring_swaps(step, lon_count)[swap])  6.25 us
    pallas_call x1, Pallas kernels, compressed(): pl.pallas_call(edge_kernel, in_specs=[smem, hbm], out_specs=[vmem] * 4, o...  5.61 us
    ppermute x1, waiting for transfers between devices, compressed(): lax.ppermute(edges[3], 'lat', swaps(lat_crosses))  3.96 us
    pallas_call x1, Pallas kernels, compressed(): pl.pallas_call(functools.partial(far_kernel, lon_count), in_specs=[smem]...  2.04 us
    ppermute x1, starting transfers between devices, compressed(): lax.ppermute(edges[3], 'lat', swaps(lat_crosses))  1.97 us
    ppermute x1, starting transfers between devices, compressed(): lax.ppermute(edges[2], 'lat', swaps(lat_pairs))  1.49 us
  transfers between devices with their start and end apart: 11, of which 4 were waited for; matrix products, arithmetic and copies ran while one was open for 2% of the time, Pallas kernels for 2%

commit v1 on v0

--- a/solution.py
+++ b/solution.py
@@ -138,15 +138,14 @@
     return ceil8(slots * rank + strip_rows(slots))
 
 
-def edge_kernel(
-    meta, state, lon_pair, lon_cross, lat_pair, lat_cross, held, edges, in_sems
-):
+def edge_columns(is_north, state, out, held, edges, sems):
     fields, levels, columns, rows = state.shape
     lists = fields * levels
+    tile = pl.ds(pl.multiple_of(jnp.where(is_north, 0, rows - POLAR), POLAR), POLAR)
 
     def copy_in(item):
         l, f = item // fields, item % fields
-        return pltpu.make_async_copy(state.at[f, l], held.at[item], in_sems.at[item])
+        return pltpu.make_async_copy(state.at[f, l, :, tile], held.at[item], sems.at[item])
 
     def start(item, carry):
         copy_in(item).start()
@@ -154,28 +153,57 @@
 
     lax.fori_loop(0, lists, start, 0)
     lane = lax.broadcasted_iota(jnp.int32, (columns, POLAR), 1)
-    lon_odd = lax.rem(meta[2], 2) == 1
-    lat_odd = lax.rem(meta[3], 2) == 1
     edges[...] = jnp.zeros(edges.shape, F32)
 
     def one(item, carry):
         copy_in(item).wait()
-        first = held[item, 0:1, :]
-        last = held[item, columns - 1 : columns, :]
-        lon_pair[pl.ds(item, 1), :] = jnp.where(lon_odd, first, last)
-        lon_cross[pl.ds(item, 1), :] = jnp.where(lon_odd, last, first)
-        north = pltpu.roll(held[item, :, 0:POLAR], item, 1)
-        south = pltpu.roll(held[item, :, rows - POLAR :], item + SOUTH + 1, 1)
-        value = jnp.where(lane == item, north, edges[...])
-        edges[...] = jnp.where(lane == SOUTH + item, south, value)
+        row = pltpu.roll(held[item], jnp.where(is_north, item, item + 1), 1)
+        edges[...] = jnp.where(lane == item, row, edges[...])
         return carry
 
     lax.fori_loop(0, lists, one, 0, unroll=5)
-    turned = edges[...].T
-    size = lat_pair.shape[0]
-    north, south = turned[0:size], turned[SOUTH : SOUTH + size]
-    lat_pair[...] = jnp.where(lat_odd, north, south)
-    lat_cross[...] = jnp.where(lat_odd, south, north)
+    out[...] = edges[...].T[0 : out.shape[0]]
+
+
+def first_edge_kernel(
+    meta, state, lon_pair, lon_cross, lat_pair, ends, held, edges, end_sems, sems
+):
+    fields, levels, columns, _ = state.shape
+    lists = fields * levels
+
+    def copy_end(item, side):
+        l, f = item // fields, item % fields
+        return pltpu.make_async_copy(
+            state.at[f, l, pl.ds(side * (columns - 8), 8), :],
+            ends.at[item, side],
+            end_sems.at[item, side],
+        )
+
+    for item in range(lists):
+        for side in range(2):
+            copy_end(item, side).start()
+    edge_columns(lax.rem(meta[3], 2) == 1, state, lat_pair, held, edges, sems)
+    lon_odd = lax.rem(meta[2], 2) == 1
+    lon_pair[...] = jnp.zeros(lon_pair.shape, F32)
+    lon_cross[...] = jnp.zeros(lon_cross.shape, F32)
+    for item in range(lists):
+        for side in range(2):
+            copy_end(item, side).wait()
+        first, last = ends[item, 0, 0:1, :], ends[item, 1, 7:8, :]
+        lon_pair[item : item + 1, :] = jnp.where(lon_odd, first, last)
+        lon_cross[item : item + 1, :] = jnp.where(lon_odd, last, first)
+
+
+def second_edge_kernel(meta, state, before, lat_cross, held, edges, sems):
+    del before
+
+    @pl.when(meta[4] == 1)
+    def _():
+        edge_columns(lax.rem(meta[3], 2) == 0, state, lat_cross, held, edges, sems)
+
+    @pl.when(meta[4] == 0)
+    def _():
+        lat_cross[...] = jnp.zeros(lat_cross.shape, F32)
 
 
 def stencil_kernel(
@@ -188,11 +216,13 @@
     lat_pair,
     lat_cross,
     diffusion,
-    cosine,
-    sine,
+    angle_cos,
+    angle_sin,
     send,
     state,
     updated,
+    cosine,
+    sine,
     own,
     *rest,
 ):
@@ -214,6 +244,14 @@
     for l in range(levels):
         for f in range(fields):
             copy_in(l, f).start()
+
+    steps = columns // STEP
+    fine_cos, fine_sin = angle_cos[steps:, :], angle_sin[steps:, :]
+    for step in range(steps):
+        span = slice(step * STEP, (step + 1) * STEP)
+        coarse_cos, coarse_sin = angle_cos[step : step + 1, :], angle_sin[step : step + 1, :]
+        cosine[span, :] = coarse_cos * fine_cos - coarse_sin * fine_sin
+        sine[span, :] = coarse_sin * fine_cos + coarse_cos * fine_sin
 
     lane = lax.broadcasted_iota(jnp.int32, (STEP, POLAR), 1)
     lowest, highest = lane == 0, lane == POLAR - 1
@@ -513,9 +551,12 @@
     is_south = lat_index == lat_count - 1
     is_polar = (lat_index == 0) | is_south
     part = jnp.where(is_south, rows // POLAR - 1, 0)
-    meta = jnp.stack([part, is_polar.astype(jnp.int32), lon_index, lat_index]).astype(jnp.int32)
+    is_crossed = jnp.where(lat_index % 2 == 1, lat_index < lat_count - 1, lat_index > 0)
+    meta = [part, is_polar, lon_index, lat_index, is_crossed]
+    meta = jnp.stack([value.astype(jnp.int32) for value in meta])
     kept = jnp.where(lat_index < lat_count // 2, cutoff[:POLAR], cutoff[POLAR:])
-    cosine, sine = phase_table(kept, jnp.arange(columns, dtype=jnp.int32), total_columns)
+    places = np.concatenate([np.arange(0, columns, STEP), np.arange(STEP)]).astype(np.int32)
+    angles = phase_table(kept, jnp.asarray(places), total_columns)
     steps = jnp.array([abs(shift) for shift, _ in ranks], jnp.int32)
     sign = np.array([[1.0 if shift > 0 else -1.0] for shift, _ in ranks], np.float32)
     turn_cos, turn_sin = phase_table(kept, steps, lon_count)
@@ -529,19 +570,32 @@
     hbm = pl.BlockSpec(memory_space=pl.ANY)
     level_sems = pltpu.SemaphoreType.DMA((levels, fields))
 
+    edge_scratch = [
+        pltpu.VMEM((lists, columns, POLAR), F32),
+        pltpu.VMEM((columns, POLAR), F32),
+    ]
+    list_sems = pltpu.SemaphoreType.DMA((lists,))
     with jax.named_scope("edges"):
         edges = pl.pallas_call(
-            edge_kernel,
+            first_edge_kernel,
             in_specs=[smem, hbm],
-            out_specs=[vmem] * 4,
-            out_shape=[shape(ceil8(lists), rows)] * 2 + [shape(ceil8(lists), columns)] * 2,
-            scratch_shapes=[
-                pltpu.VMEM((lists, columns, rows), F32),
-                pltpu.VMEM((columns, POLAR), F32),
-                pltpu.SemaphoreType.DMA((lists,)),
-            ],
+            out_specs=[vmem] * 3,
+            out_shape=[shape(ceil8(lists), rows)] * 2 + [shape(ceil8(lists), columns)],
+            scratch_shapes=[pltpu.VMEM((lists, 2, 8, rows), F32)]
+            + edge_scratch
+            + [pltpu.SemaphoreType.DMA((lists, 2)), list_sems],
             compiler_params=params,
         )(meta, model_state)
+    with jax.named_scope("second_edges"):
+        second_edge = pl.pallas_call(
+            second_edge_kernel,
+            in_specs=[smem, hbm, hbm],
+            out_specs=vmem,
+            out_shape=shape(ceil8(lists), columns),
+            scratch_shapes=edge_scratch + [list_sems],
+            compiler_params=params,
+            cost_estimate=cost(0, 4 * lists * columns * POLAR),
+        )(meta, model_state, edges[2])
 
     with jax.named_scope("halo"):
         lon_pairs, lon_crosses = ring_swaps(1, lon_count)
@@ -551,16 +605,19 @@
             lax.ppermute(edges[0], "lon", lon_pairs),
             lax.ppermute(edges[1], "lon", lon_crosses),
             lax.ppermute(edges[2], "lat", swaps(lat_pairs)),
-            lax.ppermute(edges[3], "lat", swaps(lat_crosses)),
+            lax.ppermute(second_edge, "lat", swaps(lat_crosses)),
         ]
 
     sizes = [payload_rows(rank, lists) for _, rank in ranks]
     with jax.named_scope("stencil"):
-        updated, own, *outgoing = pl.pallas_call(
+        updated, cosine, sine, own, *outgoing = pl.pallas_call(
             functools.partial(stencil_kernel, lon_count),
             in_specs=[smem] * 3 + [vmem] * 8 + [hbm],
-            out_specs=[hbm] + [vmem] * (1 + len(ranks)),
-            out_shape=[whole_state, shape(16, rows)] + [shape(size, rows) for size in sizes],
+            out_specs=[hbm] + [vmem] * (3 + len(ranks)),
+            out_shape=[whole_state]
+            + [shape(columns, POLAR)] * 2
+            + [shape(16, rows)]
+            + [shape(size, rows) for size in sizes],
             scratch_shapes=[
                 pltpu.VMEM((levels, fields, columns + 16, rows), F32),
                 pltpu.VMEM((levels, fields, columns, rows), F32),
@@ -579,8 +636,7 @@
             strip_list,
             *halos,
             diffusion,
-            cosine,
-            sine,
+            *angles,
             send,
             model_state,
         )

time: 57.7 us -> 61.5 us (1.066)
  Pallas kernels: 22.5 us -> 26.3 us
  other arithmetic: 1.18 us -> 0.32 us
  waiting for transfers between devices: 21.9 us -> 22.7 us
    pallas_call x1 -> x2, Pallas kernels: 5.61 us -> 9.37 us  [the longest x1 5.04 us: compressed(): pl.pallas_call(first_edge_kernel, in_specs=[smem, hbm], out_specs=[vmem]...]
    sin x1, other arithmetic: 0.97 us -> 0.19 us  [phase_table(): return (jnp.cos(angle), jnp.sin(angle))]
    ppermute x1, waiting for transfers between devices: 3.96 us -> 4.73 us  [compressed(): lax.ppermute(second_edge, 'lat', swaps(lat_crosses))]
  transfers between devices with their start and end apart: 11 -> 11, of which waited for: 4 -> 4; matrix products, arithmetic and copies ran while one was open for 2% -> 1% of each run, Pallas kernels for 2% -> 9%
where the time goes in v1:
time: 61.5 us; the launch traced here: 60.9 us
  Pallas kernels  26.3 us (43%)
  waiting for transfers between devices  22.7 us (37%)
  starting transfers between devices  10.3 us (17%)
  between operations  0.87 us (1%)
    ppermute x7, waiting for transfers between devices, exchange(): return lax.ppermute(payload, 'lon', ring_swaps(step, lon_count)[swap])  17.9 us
    pallas_call x1, Pallas kernels, compressed(): pl.pallas_call(functools.partial(stencil_kernel, lon_count), in_specs=[sm...  13.6 us
    ppermute x7, starting transfers between devices, exchange(): return lax.ppermute(payload, 'lon', ring_swaps(step, lon_count)[swap])  6.24 us
    pallas_call x1, Pallas kernels, compressed(): pl.pallas_call(first_edge_kernel, in_specs=[smem, hbm], out_specs=[vmem]...  5.04 us
    ppermute x1, waiting for transfers between devices, compressed(): lax.ppermute(second_edge, 'lat', swaps(lat_crosses))  4.73 us
    pallas_call x1, Pallas kernels, compressed(): pl.pallas_call(second_edge_kernel, in_specs=[smem, hbm, hbm], out_specs=v...  4.34 us
    pallas_call x1, Pallas kernels, compressed(): pl.pallas_call(functools.partial(far_kernel, lon_count), in_specs=[smem]...  2.03 us
    ppermute x1, starting transfers between devices, compressed(): lax.ppermute(second_edge, 'lat', swaps(lat_crosses))  1.99 us
  transfers between devices with their start and end apart: 11, of which 4 were waited for; matrix products, arithmetic and copies ran while one was open for 1% of the time, Pallas kernels for 9%

profile of v1, /device:TPU:12, one launch (start us, length us, event | category | flops | bytes accessed | tf_op | source)
XLA Modules:
  0.0 60.9 jit_solution(3295645074820058024)
XLA Ops:
  0.7 0.1 stack.31.meta
  0.8 0.0 copy-start.6
  0.8 0.0 copy-start.7
  0.8 0.0 copy-start.5
  0.8 0.0 copy-start.2
  0.8 0.0 copy-start.4
  0.8 5.0 %edges.1 = (f32[24,256]{1,0:T(8,128)S(1)}, f32[24,256]{1,0:T(8,128)S(1)}, f32[24,448]{1,0:T(8,128)S(1)}) custom-call(s32[5]{0:T(128)S(1)} %stack.31.meta, f32[5,4,448,256]{3,2,1,0:T(8,128)} %state.5), custom_call_target="tpu_custom_call" | custom-call | tf_op jit(solution)/shard_map/edges/pallas_call | solution.py:579
  5.9 0.1 collective-permute-start
  5.9 0.6 collective-permute-start.1
  6.5 1.5 %collective-permute-start.2 = (f32[24,448]{1,0:T(8,128)S(1)}, f32[24,448]{1,0:T(8,128)S(1)}, u32[]{:S(2)}, u32[]{:S(2)}) collective-permute-start(f32[24,448]{1,0:T(8,128)S(1)} %get-tuple-element.26.before), channel_id=1, source_target_pairs={{0,8},{8,0},{16,24},{24,16},{1,9},{9,1},{17,25},{25,17},{2,10},{10... | collective-permute-start | bytes 129032 | tf_op jit(solution)/shard_map/halo/ppermute | solution.py:607
  8.0 4.3 %second_edges.1 = f32[24,448]{1,0:T(8,128)S(1)} custom-call(s32[5]{0:T(128)S(1)} %stack.31.meta, f32[5,4,448,256]{3,2,1,0:T(8,128)} %state.5, f32[24,448]{1,0:T(8,128)S(1)} %get-tuple-element.26.before), custom_call_target="tpu_custom_call" | custom-call | bytes 4587520 | tf_op jit(solution)/shard_map/second_edges/pallas_call | solution.py:590
  12.3 2.0 %collective-permute-start.3 = (f32[24,448]{1,0:T(8,128)S(1)}, f32[24,448]{1,0:T(8,128)S(1)}, u32[]{:S(2)}, u32[]{:S(2)}) collective-permute-start(f32[24,448]{1,0:T(8,128)S(1)} %second_edges.1), channel_id=1, source_target_pairs={{8,16},{16,8},{9,17},{17,9},{10,18},{18,10},{11,19},{19,11},{12,20... | collective-permute-start | bytes 129032 | tf_op jit(solution)/shard_map/halo/ppermute | solution.py:608
  14.4 0.2 fusion.4
  14.6 0.1 fusion.10
  14.7 0.1 copy.24.strips
  14.8 0.1 copy.25.begins
  14.9 0.1 reshape.14.coupling
  15.0 4.7 %collective-permute-done.3.lat_cross = f32[24,448]{1,0:T(8,128)S(1)} collective-permute-done((f32[24,448]{1,0:T(8,128)S(1)}, f32[24,448]{1,0:T(8,128)S(1)}, u32[]{:S(2)}, u32[]{:S(2)}) %collective-permute-start.3) | collective-permute-done | bytes 43040 | tf_op jit(solution)/shard_map/halo/ppermute | solution.py:608
  19.7 0.0 collective-permute-done.2.lat_pair
  19.7 13.6 %stencil.1 = (f32[5,4,448,256]{3,2,1,0:T(8,128)}, f32[448,128]{1,0:T(8,128)S(1)}, f32[448,128]{1,0:T(8,128)S(1)}, f32[16,256]{1,0:T(8,128)S(1)}, f32[296,256]{1,...) custom-call(s32[5]{0:T(128)S(1)} %stack.31.meta, ...), custom_call_target="tpu_custom_call" | custom-call | tf_op jit(solution)/shard_map/stencil/pallas_call | solution.py:613
  33.3 0.1 collective-permute-start.4
  33.4 2.2 %collective-permute-start.9 = (f32[96,256]{1,0:T(8,128)S(1)}, f32[96,256]{1,0:T(8,128)S(1)}, u32[]{:S(2)}, u32[]{:S(2)}) collective-permute-start(f32[96,256]{1,0:T(8,128)S(1)} %get-tuple-element.40), channel_id=1, source_target_pairs={{1,4},{4,1},{3,6},{6,3},{5,0},{0,5},{7,2},{2,7},{9,12},{12,9},{11,... | collective-permute-start | bytes 294920 | tf_op jit(solution)/shard_map/exchange/ppermute | solution.py:647
  35.6 0.8 %collective-permute-start.10 = (f32[96,256]{1,0:T(8,128)S(1)}, f32[96,256]{1,0:T(8,128)S(1)}, u32[]{:S(2)}, u32[]{:S(2)}) collective-permute-start(f32[96,256]{1,0:T(8,128)S(1)} %get-tuple-element.41), channel_id=1, source_target_pairs={{0,4},{4,0},{1,5},{5,1},{2,6},{6,2},{3,7},{7,3},{8,12},{12,8},{9,1... | collective-permute-start | bytes 294920 | tf_op jit(solution)/shard_map/exchange/ppermute | solution.py:647
  36.4 3.1 %collective-permute-start.5 = (f32[112,256]{1,0:T(8,128)S(1)}, f32[112,256]{1,0:T(8,128)S(1)}, u32[]{:S(2)}, u32[]{:S(2)}) collective-permute-start(f32[112,256]{1,0:T(8,128)S(1)} %get-tuple-element.32), channel_id=1, source_target_pairs={{0,2},{2,0},{1,3},{3,1},{4,6},{6,4},{5,7},{7,5},{8,10},{10,8},{9,1... | collective-permute-start | bytes 344072 | tf_op jit(solution)/shard_map/exchange/ppermute | solution.py:647
  39.5 0.6 %near.3 = (f32[8,448,128]{2,1,0:T(8,128)S(1)}, f32[8,32,256]{2,1,0:T(8,128)S(1)}, f32[112,256]{1,0:T(8,128)S(1)}, f32[96,256]{1,0:T(8,128)S(1)}) custom-call(s32[5]{0:T(128)S(1)} %stack.31.meta, f32[448,128]{1,0:T(8,128)S(1)} %get-tuple-element.27.cosine, f32[448,128]{1,0:T(8,128)S(1)} %get-tuple-element.28.sine, ...), custom_call_target="tpu_custom_call", output_to_operand_aliasing={{2}: (6, {}), {3}: (7, {})} | custom-call | flops 2466250752 | bytes 3670016 | tf_op jit(solution)/shard_map/near/pallas_call | solution.py:657
  40.2 0.0 copy-start.1
  40.2 0.0 copy-start.3
  40.2 9.1 %collective-permute-done.5.rest_1_ = f32[112,256]{1,0:T(8,128)S(1)} collective-permute-done((f32[112,256]{1,0:T(8,128)S(1)}, f32[112,256]{1,0:T(8,128)S(1)}, u32[]{:S(2)}, u32[]{:S(2)}) %collective-permute-start.5) | collective-permute-done | bytes 114720 | tf_op jit(solution)/shard_map/exchange/ppermute | solution.py:647
  49.3 0.7 %near_rest.1 = (f32[12,448,128]{2,1,0:T(8,128)S(1)}, f32[12,32,256]{2,1,0:T(8,128)S(1)}, f32[296,256]{1,0:T(8,128)S(1)}, f32[112,256]{1,0:T(8,128)S(1)}) custom-call(s32[5]{0:T(128)S(1)} %stack.31.meta, f32[448,128]{1,0:T(8,128)S(1)} %get-tuple-element.27.cosine, ...), custom_call_target="tpu_custom_call", output_to_operand_aliasing={{2}: (6, {}), {3}: (7, {})} | custom-call | flops 3699376128 | bytes 5505024 | tf_op jit(solution)/shard_map/near_rest/pallas_call | solution.py:657
  50.0 7.4 %collective-permute-done.8.rest_4_ = f32[96,256]{1,0:T(8,128)S(1)} collective-permute-done((f32[96,256]{1,0:T(8,128)S(1)}, f32[96,256]{1,0:T(8,128)S(1)}, u32[]{:S(2)}, u32[]{:S(2)}) %collective-permute-start.8) | collective-permute-done | bytes 98336 | tf_op jit(solution)/shard_map/late_exchange/ppermute | solution.py:647
  57.4 1.4 %collective-permute-done.7.rest_3_ = f32[112,256]{1,0:T(8,128)S(1)} collective-permute-done((f32[112,256]{1,0:T(8,128)S(1)}, f32[112,256]{1,0:T(8,128)S(1)}, u32[]{:S(2)}, u32[]{:S(2)}) %collective-permute-start.7) | collective-permute-done | bytes 114720 | tf_op jit(solution)/shard_map/late_exchange/ppermute | solution.py:647
  58.8 2.0 %far.2 = (f32[5,4,448,256]{3,2,1,0:T(8,128)}, f32[1,5,4,2048]{3,2,1,0:T(4,128)}) custom-call(s32[5]{0:T(128)S(1)} %stack.31.meta, s32[8,2]{1,0:T(8,128)S(1)} %copy.25.begins, f32[448,128]{1,0:T(8,128)S(1)} %get-tuple-element.27.cosine, f32[448,128]{1,0:T(8,128)S(1)} %get-tuple-element.28.sine, ...), custom_call_target="tpu_custom_call", output_to_operand_aliasing={{0}: (19, {})} | custom-call | tf_op jit(solution)/shard_map/far/pallas_call | solution.py:685
  (29 shorter events, 0.1 us)
Async XLA Ops:
  0.7 13.6 %copy-start.8 = (s32[256]{0:T(256)S(1)}, s32[256]{0:T(256)}, u32[]{:S(2)}) copy-start(s32[256]{0:T(256)} %param.16) | copy-start | bytes 3076
  0.7 13.6 %copy-start.9 = (s32[44]{0:T(128)S(1)}, s32[44]{0:T(128)}, u32[]{:S(2)}) copy-start(s32[44]{0:T(128)} %constant.80.clone) | copy-start | bytes 532
  0.7 13.8 %copy-start.10 = (f32[7]{0:T(128)S(1)}, f32[7]{0:T(128)}, u32[]{:S(2)}) copy-start(f32[7]{0:T(128)} %constant.88) | copy-start | bytes 88
  0.7 13.8 %copy-start.11 = (s32[7]{0:T(128)S(1)}, s32[7]{0:T(128)}, u32[]{:S(2)}) copy-start(s32[7]{0:T(128)} %constant.81.clone) | copy-start | bytes 88
  0.8 13.9 %copy-start.6 = (s32[8,4]{0,1:T(4,128)S(1)}, s32[8,4]{0,1:T(4,128)}, u32[]{:S(2)}) copy-start(s32[8,4]{0,1:T(4,128)} %param.17) | copy-start | bytes 388
  0.8 14.0 %copy-start.7 = (s32[1,8,2]{1,2,0:T(2,128)S(1)}, s32[1,8,2]{1,2,0:T(2,128)}, u32[]{:S(2)}) copy-start(s32[1,8,2]{1,2,0:T(2,128)} %param.18) | copy-start | bytes 196
  0.8 14.1 %copy-start.5 = (f32[4,5,5]{2,0,1:T(4,128)S(1)}, f32[4,5,5]{2,0,1:T(4,128)}, u32[]{:S(2)}) copy-start(f32[4,5,5]{2,0,1:T(4,128)} %param.15) | copy-start | bytes 1204
  0.8 18.9 %copy-start.2 = (bf16[144,448]{1,0:T(8,128)(2,1)S(1)}, bf16[144,448]{1,0:T(8,128)(2,1)}, u32[]{:S(2)}) copy-start(bf16[144,448]{1,0:T(8,128)(2,1)} %constant.78.clone.send) | copy-start | bytes 387076
  0.8 18.9 %copy-start.4 = (f32[2,256]{1,0:T(2,128)S(1)}, f32[2,256]{1,0:T(2,128)}, u32[]{:S(2)}) copy-start(f32[2,256]{1,0:T(2,128)} %diffusion.1) | copy-start | bytes 6148
  5.9 9.1 %collective-permute-start = (f32[24,256]{1,0:T(8,128)S(1)}, f32[24,256]{1,0:T(8,128)S(1)}, u32[]{:S(2)}, u32[]{:S(2)}) collective-permute-start(f32[24,256]{1,0:T(8,128)S(1)} %get-tuple-element.24), channel_id=1, source_target_pairs={{0,1},{1,0},{2,3},{3,2},{4,5},{5,4},{6,7},{7,6},{8,9},{9,8},{10,11... | collective-permute-start | bytes 73736 | tf_op jit(solution)/shard_map/halo/ppermute | solution.py:605
  5.9 9.0 %collective-permute-start.1 = (f32[24,256]{1,0:T(8,128)S(1)}, f32[24,256]{1,0:T(8,128)S(1)}, u32[]{:S(2)}, u32[]{:S(2)}) collective-permute-start(f32[24,256]{1,0:T(8,128)S(1)} %get-tuple-element.25), channel_id=1, source_target_pairs={{1,2},{2,1},{3,4},{4,3},{5,6},{6,5},{7,0},{0,7},{9,10},{10,9},{11,... | collective-permute-start | bytes 73736 | tf_op jit(solution)/shard_map/halo/ppermute | solution.py:606
  6.5 33.1 %copy-start = (bf16[960,224]{1,0:T(8,128)(2,1)S(1)}, bf16[960,224]{1,0:T(8,128)(2,1)}, u32[]{:S(2)}) copy-start(bf16[960,224]{1,0:T(8,128)(2,1)} %constant.77.clone.near) | copy-start | bytes 1290244
  6.5 13.2 %collective-permute-start.2 = (f32[24,448]{1,0:T(8,128)S(1)}, f32[24,448]{1,0:T(8,128)S(1)}, u32[]{:S(2)}, u32[]{:S(2)}) collective-permute-start(f32[24,448]{1,0:T(8,128)S(1)} %get-tuple-element.26.before), channel_id=1, source_target_pairs={{0,8},{8,0},{16,24},{24,16},{1,9},{9,1},{17,25},{25,17},{2,10},{10... | collective-permute-start | bytes 129032 | tf_op jit(solution)/shard_map/halo/ppermute | solution.py:607
  12.3 7.4 %collective-permute-start.3 = (f32[24,448]{1,0:T(8,128)S(1)}, f32[24,448]{1,0:T(8,128)S(1)}, u32[]{:S(2)}, u32[]{:S(2)}) collective-permute-start(f32[24,448]{1,0:T(8,128)S(1)} %second_edges.1), channel_id=1, source_target_pairs={{8,16},{16,8},{9,17},{17,9},{10,18},{18,10},{11,19},{19,11},{12,20... | collective-permute-start | bytes 129032 | tf_op jit(solution)/shard_map/halo/ppermute | solution.py:608
  33.3 16.0 %collective-permute-start.4 = (f32[296,256]{1,0:T(8,128)S(1)}, f32[296,256]{1,0:T(8,128)S(1)}, u32[]{:S(2)}, u32[]{:S(2)}) collective-permute-start(f32[296,256]{1,0:T(8,128)S(1)} %get-tuple-element.31), channel_id=1, source_target_pairs={{0,1},{1,0},{2,3},{3,2},{4,5},{5,4},{6,7},{7,6},{8,9},{9,8},{10,11... | collective-permute-start | bytes 909320 | tf_op jit(solution)/shard_map/exchange/ppermute | solution.py:647
  33.4 16.5 %collective-permute-start.9 = (f32[96,256]{1,0:T(8,128)S(1)}, f32[96,256]{1,0:T(8,128)S(1)}, u32[]{:S(2)}, u32[]{:S(2)}) collective-permute-start(f32[96,256]{1,0:T(8,128)S(1)} %get-tuple-element.40), channel_id=1, source_target_pairs={{1,4},{4,1},{3,6},{6,3},{5,0},{0,5},{7,2},{2,7},{9,12},{12,9},{11,... | collective-permute-start | bytes 294920 | tf_op jit(solution)/shard_map/exchange/ppermute | solution.py:647
  35.6 14.4 %collective-permute-start.10 = (f32[96,256]{1,0:T(8,128)S(1)}, f32[96,256]{1,0:T(8,128)S(1)}, u32[]{:S(2)}, u32[]{:S(2)}) collective-permute-start(f32[96,256]{1,0:T(8,128)S(1)} %get-tuple-element.41), channel_id=1, source_target_pairs={{0,4},{4,0},{1,5},{5,1},{2,6},{6,2},{3,7},{7,3},{8,12},{12,8},{9,1... | collective-permute-start | bytes 294920 | tf_op jit(solution)/shard_map/exchange/ppermute | solution.py:647
  36.4 12.9 %collective-permute-start.5 = (f32[112,256]{1,0:T(8,128)S(1)}, f32[112,256]{1,0:T(8,128)S(1)}, u32[]{:S(2)}, u32[]{:S(2)}) collective-permute-start(f32[112,256]{1,0:T(8,128)S(1)} %get-tuple-element.32), channel_id=1, source_target_pairs={{0,2},{2,0},{1,3},{3,1},{4,6},{6,4},{5,7},{7,5},{8,10},{10,8},{9,1... | collective-permute-start | bytes 344072 | tf_op jit(solution)/shard_map/exchange/ppermute | solution.py:647
  39.5 19.3 %collective-permute-start.6 = (f32[296,256]{1,0:T(8,128)S(1)}, f32[296,256]{1,0:T(8,128)S(1)}, u32[]{:S(2)}, u32[]{:S(2)}) collective-permute-start(f32[296,256]{1,0:T(8,128)S(1)} %get-tuple-element.34), channel_id=1, source_target_pairs={{1,2},{2,1},{3,4},{4,3},{5,6},{6,5},{7,0},{0,7},{9,10},{10,9},{11,... | collective-permute-start | bytes 909320 | tf_op jit(solution)/shard_map/exchange/ppermute | solution.py:647
  40.2 18.6 %copy-start.1 = (bf16[448,240]{1,0:T(8,128)(2,1)S(1)}, bf16[448,240]{1,0:T(8,128)(2,1)}, u32[]{:S(2)}) copy-start(bf16[448,240]{1,0:T(8,128)(2,1)} %constant.79.clone.far) | copy-start | bytes 645124
  40.2 18.6 %copy-start.3 = (bf16[128,512]{1,0:T(8,128)(2,1)S(1)}, bf16[128,512]{1,0:T(8,128)(2,1)}, u32[]{:S(2)}) copy-start(bf16[128,512]{1,0:T(8,128)(2,1)} %constant.83.clone.hats) | copy-start | bytes 393220
  49.3 8.1 %collective-permute-start.8 = (f32[96,256]{1,0:T(8,128)S(1)}, f32[96,256]{1,0:T(8,128)S(1)}, u32[]{:S(2)}, u32[]{:S(2)}) collective-permute-start(f32[96,256]{1,0:T(8,128)S(1)} %get-tuple-element.39), channel_id=1, source_target_pairs={{0,3},{3,0},{2,5},{5,2},{4,7},{7,4},{6,1},{1,6},{8,11},{11,8},{10,... | collective-permute-start | bytes 294920 | tf_op jit(solution)/shard_map/late_exchange/ppermute | solution.py:647
  49.3 9.5 %collective-permute-start.7 = (f32[112,256]{1,0:T(8,128)S(1)}, f32[112,256]{1,0:T(8,128)S(1)}, u32[]{:S(2)}, u32[]{:S(2)}) collective-permute-start(f32[112,256]{1,0:T(8,128)S(1)} %get-tuple-element.38), channel_id=1, source_target_pairs={{2,4},{4,2},{3,5},{5,3},{6,0},{0,6},{7,1},{1,7},{10,12},{12,10},{1... | collective-permute-start | bytes 344072 | tf_op jit(solution)/shard_map/late_exchange/ppermute | solution.py:647

commit v2 on v0

--- a/solution.py
+++ b/solution.py
@@ -19,7 +19,7 @@
 SPLIT_RANK = 14
 STEP = 16
 HELD = 80
-EARLY_LISTS = 8
+NEAR_LISTS = (6, 6, 8)
 QUICK = (0, 2)
 LATE = (3, 4)
 SOUTH = 64
@@ -142,35 +142,29 @@
     meta, state, lon_pair, lon_cross, lat_pair, lat_cross, held, edges, in_sems
 ):
     fields, levels, columns, rows = state.shape
-    lists = fields * levels
-
-    def copy_in(item):
-        l, f = item // fields, item % fields
-        return pltpu.make_async_copy(state.at[f, l], held.at[item], in_sems.at[item])
-
-    def start(item, carry):
-        copy_in(item).start()
-        return carry
-
-    lax.fori_loop(0, lists, start, 0)
+    copies = [
+        pltpu.make_async_copy(state.at[f], held.at[f], in_sems.at[f]) for f in range(fields)
+    ]
+    for copy in copies:
+        copy.start()
     lane = lax.broadcasted_iota(jnp.int32, (columns, POLAR), 1)
     lon_odd = lax.rem(meta[2], 2) == 1
     lat_odd = lax.rem(meta[3], 2) == 1
     edges[...] = jnp.zeros(edges.shape, F32)
 
-    def one(item, carry):
-        copy_in(item).wait()
-        first = held[item, 0:1, :]
-        last = held[item, columns - 1 : columns, :]
-        lon_pair[pl.ds(item, 1), :] = jnp.where(lon_odd, first, last)
-        lon_cross[pl.ds(item, 1), :] = jnp.where(lon_odd, last, first)
-        north = pltpu.roll(held[item, :, 0:POLAR], item, 1)
-        south = pltpu.roll(held[item, :, rows - POLAR :], item + SOUTH + 1, 1)
-        value = jnp.where(lane == item, north, edges[...])
-        edges[...] = jnp.where(lane == SOUTH + item, south, value)
-        return carry
-
-    lax.fori_loop(0, lists, one, 0, unroll=5)
+    for f, copy in enumerate(copies):
+        copy.wait()
+        for l in range(levels):
+            item = l * fields + f
+            first = held[f, l, 0:1, :]
+            last = held[f, l, columns - 1 : columns, :]
+            lon_pair[item : item + 1, :] = jnp.where(lon_odd, first, last)
+            lon_cross[item : item + 1, :] = jnp.where(lon_odd, last, first)
+            north = held[f, l, :, 0:POLAR]
+            north = pltpu.roll(north, item, 1) if item else north
+            south = pltpu.roll(held[f, l, :, rows - POLAR :], item + SOUTH + 1, 1)
+            value = jnp.where(lane == item, north, edges[...])
+            edges[...] = jnp.where(lane == SOUTH + item, south, value)
     turned = edges[...].T
     size = lat_pair.shape[0]
     north, south = turned[0:size], turned[SOUTH : SOUTH + size]
@@ -188,11 +182,13 @@
     lat_pair,
     lat_cross,
     diffusion,
-    cosine,
-    sine,
+    angle_cos,
+    angle_sin,
     send,
     state,
     updated,
+    cosine,
+    sine,
     own,
     *rest,
 ):
@@ -214,6 +210,14 @@
     for l in range(levels):
         for f in range(fields):
             copy_in(l, f).start()
+
+    steps = columns // STEP
+    fine_cos, fine_sin = angle_cos[steps:, :], angle_sin[steps:, :]
+    for step in range(steps):
+        span = slice(step * STEP, (step + 1) * STEP)
+        coarse_cos, coarse_sin = angle_cos[step : step + 1, :], angle_sin[step : step + 1, :]
+        cosine[span, :] = coarse_cos * fine_cos - coarse_sin * fine_sin
+        sine[span, :] = coarse_sin * fine_cos + coarse_cos * fine_sin
 
     lane = lax.broadcasted_iota(jnp.int32, (STEP, POLAR), 1)
     lowest, highest = lane == 0, lane == POLAR - 1
@@ -374,14 +378,15 @@
                 moments[item, part * 16 : (part + 1) * 16, :] = total[half:, :]
             return carry
 
-        lax.fori_loop(0, lists, one, 0, unroll=4)
+        lax.fori_loop(0, lists, one, 0, unroll=2)
 
 
 def far_kernel(count, meta, begins, cosine, sine, turn, far, hats, own, *rest):
     ranks = shift_ranks(count)
     payloads = rest[: len(ranks)]
-    near_parts = (rest[len(ranks) : len(ranks) + 2], rest[len(ranks) + 2 : len(ranks) + 4])
-    _, out, boundary, filtered, arrived, sums, sems = rest[len(ranks) + 4 :]
+    after = len(ranks) + 2 * len(NEAR_LISTS)
+    near_parts = [rest[at : at + 2] for at in range(len(ranks), after, 2)]
+    _, out, boundary, filtered, arrived, sums, sems = rest[after:]
     fields, levels = out.shape[0:2]
     lists = fields * levels
     each = strip_rows(lists)
@@ -444,7 +449,7 @@
                 copy_out(at).start()
                 return carry
 
-            lax.fori_loop(0, near.shape[0], one, 0, unroll=4)
+            lax.fori_loop(0, near.shape[0], one, 0, unroll=2)
             begin += near.shape[0]
 
     sums[...] = jnp.zeros(sums.shape, F32)
@@ -515,7 +520,8 @@
     part = jnp.where(is_south, rows // POLAR - 1, 0)
     meta = jnp.stack([part, is_polar.astype(jnp.int32), lon_index, lat_index]).astype(jnp.int32)
     kept = jnp.where(lat_index < lat_count // 2, cutoff[:POLAR], cutoff[POLAR:])
-    cosine, sine = phase_table(kept, jnp.arange(columns, dtype=jnp.int32), total_columns)
+    places = np.concatenate([np.arange(0, columns, STEP), np.arange(STEP)]).astype(np.int32)
+    angles = phase_table(kept, jnp.asarray(places), total_columns)
     steps = jnp.array([abs(shift) for shift, _ in ranks], jnp.int32)
     sign = np.array([[1.0 if shift > 0 else -1.0] for shift, _ in ranks], np.float32)
     turn_cos, turn_sin = phase_table(kept, steps, lon_count)
@@ -536,9 +542,9 @@
             out_specs=[vmem] * 4,
             out_shape=[shape(ceil8(lists), rows)] * 2 + [shape(ceil8(lists), columns)] * 2,
             scratch_shapes=[
-                pltpu.VMEM((lists, columns, rows), F32),
+                pltpu.VMEM((fields, levels, columns, rows), F32),
                 pltpu.VMEM((columns, POLAR), F32),
-                pltpu.SemaphoreType.DMA((lists,)),
+                pltpu.SemaphoreType.DMA((fields,)),
             ],
             compiler_params=params,
         )(meta, model_state)
@@ -556,11 +562,14 @@
 
     sizes = [payload_rows(rank, lists) for _, rank in ranks]
     with jax.named_scope("stencil"):
-        updated, own, *outgoing = pl.pallas_call(
+        updated, cosine, sine, own, *outgoing = pl.pallas_call(
             functools.partial(stencil_kernel, lon_count),
             in_specs=[smem] * 3 + [vmem] * 8 + [hbm],
-            out_specs=[hbm] + [vmem] * (1 + len(ranks)),
-            out_shape=[whole_state, shape(16, rows)] + [shape(size, rows) for size in sizes],
+            out_specs=[hbm] + [vmem] * (3 + len(ranks)),
+            out_shape=[whole_state]
+            + [shape(columns, POLAR)] * 2
+            + [shape(16, rows)]
+            + [shape(size, rows) for size in sizes],
             scratch_shapes=[
                 pltpu.VMEM((levels, fields, columns + 16, rows), F32),
                 pltpu.VMEM((levels, fields, columns, rows), F32),
@@ -579,8 +588,7 @@
             strip_list,
             *halos,
             diffusion,
-            cosine,
-            sine,
+            *angles,
             send,
             model_state,
         )
@@ -616,22 +624,30 @@
         )(meta, cosine, sine, middle, near, updated, *passed)
         return results[:2], results[2:]
 
-    with jax.named_scope("near"):
-        near_first, passed = near_part(0, EARLY_LISTS, [outgoing[index] for index in LATE])
-    with jax.named_scope("late_exchange"):
-        for index, payload in zip(LATE, passed):
-            incoming[index] = exchange(index, payload)
-    with jax.named_scope("near_rest"):
-        near_last, passed = near_part(EARLY_LISTS, lists, [incoming[index] for index in QUICK])
-        incoming.update(zip(QUICK, passed))
+    near_parts = []
+    begin = 0
+    for index, count in enumerate(NEAR_LISTS):
+        late, quick = LATE[index : index + 1], QUICK[index - 1 : index] if index else ()
+        with jax.named_scope("near"):
+            results, passed = near_part(
+                begin,
+                begin + count,
+                [outgoing[swap] for swap in late] + [incoming[swap] for swap in quick],
+            )
+        near_parts += results
+        begin += count
+        with jax.named_scope("late_exchange"):
+            for swap, payload in zip(late, passed):
+                incoming[swap] = exchange(swap, payload)
+        incoming.update(zip(quick, passed[len(late) :]))
 
     with jax.named_scope("far"):
         advanced, boundary = pl.pallas_call(
             functools.partial(far_kernel, lon_count),
-            in_specs=[smem] * 2 + [vmem] * (10 + len(ranks)) + [hbm],
+            in_specs=[smem] * 2 + [vmem] * (6 + len(ranks) + len(near_parts)) + [hbm],
             out_specs=[hbm, vmem],
             out_shape=[whole_state, shape(1, fields, levels, NB)],
-            input_output_aliases={12 + len(ranks): 0},
+            input_output_aliases={8 + len(ranks) + len(near_parts): 0},
             scratch_shapes=[
                 pltpu.VMEM((lists, columns, POLAR), F32),
                 pltpu.VMEM((lists, HELD, rows), F32),
@@ -649,8 +665,7 @@
             hats,
             own,
             *[incoming[index] for index in range(len(ranks))],
-            *near_first,
-            *near_last,
+            *near_parts,
             updated,
         )
     return advanced, boundary

time: 57.7 us -> 57.3 us (level)
  starting transfers between devices: 10.3 us -> 11.5 us
  other arithmetic: 1.18 us -> 0.39 us
    ppermute x7, waiting for transfers between devices: 17.9 us -> 16.7 us  [exchange(): return lax.ppermute(payload, 'lon', ring_swaps(step, lon_count)[swap])]
    ppermute x7, starting transfers between devices: 6.25 us -> 7.4 us  [exchange(): return lax.ppermute(payload, 'lon', ring_swaps(step, lon_count)[swap])]
    sin x1, other arithmetic: 0.97 us -> 0.19 us  [phase_table(): return (jnp.cos(angle), jnp.sin(angle))]
    pallas_call x1, Pallas kernels: 5.61 us -> 4.95 us  [compressed(): pl.pallas_call(edge_kernel, in_specs=[smem, hbm], out_specs=[vmem] * 4, o...]
    pallas_call x2 -> x3, Pallas kernels: 1.28 us -> 1.82 us  [near_part(): pl.pallas_call(functools.partial(near_kernel, begin, len(passed)), in_spe...]
  transfers between devices with their start and end apart: 11 -> 11, of which waited for: 4 -> 4; matrix products, arithmetic and copies ran while one was open for 2% -> 1% of each run, Pallas kernels for 2% -> 3%
where the time goes in v2:
time: 57.3 us; the launch traced here: 57.1 us
  Pallas kernels  22.4 us (39%)
  waiting for transfers between devices  21.7 us (38%)
  starting transfers between devices  11.5 us (20%)
  between operations  0.86 us (2%)
    ppermute x7, waiting for transfers between devices, exchange(): return lax.ppermute(payload, 'lon', ring_swaps(step, lon_count)[swap])  16.7 us
    pallas_call x1, Pallas kernels, compressed(): pl.pallas_call(functools.partial(stencil_kernel, lon_count), in_specs=[sm...  13.6 us
    ppermute x7, starting transfers between devices, exchange(): return lax.ppermute(payload, 'lon', ring_swaps(step, lon_count)[swap])  7.4 us
    pallas_call x1, Pallas kernels, compressed(): pl.pallas_call(edge_kernel, in_specs=[smem, hbm], out_specs=[vmem] * 4, o...  4.95 us
    ppermute x1, waiting for transfers between devices, compressed(): lax.ppermute(edges[3], 'lat', swaps(lat_crosses))  4.46 us
    pallas_call x1, Pallas kernels, compressed(): pl.pallas_call(functools.partial(far_kernel, lon_count), in_specs=[smem]...  2.04 us
    ppermute x1, starting transfers between devices, compressed(): lax.ppermute(edges[3], 'lat', swaps(lat_crosses))  1.97 us
    pallas_call x3, Pallas kernels, near_part(): pl.pallas_call(functools.partial(near_kernel, begin, len(passed)), in_spe...  1.82 us
  transfers between devices with their start and end apart: 11, of which 4 were waited for; matrix products, arithmetic and copies ran while one was open for 1% of the time, Pallas kernels for 3%

profile of v2, /device:TPU:12, one launch (start us, length us, event | category | flops | bytes accessed | tf_op | source)
XLA Modules:
  0.0 57.1 jit_solution(11340557756644192669)
XLA Ops:
  0.6 0.0 copy-start.9
  0.6 0.0 copy-start.2
  0.7 0.1 pad_add_fusion.meta
  0.8 5.0 %edges.1 = (f32[24,256]{1,0:T(8,128)S(1)}, f32[24,256]{1,0:T(8,128)S(1)}, f32[24,448]{1,0:T(8,128)S(1)}, f32[24,448]{1,0:T(8,128)S(1)}) custom-call(s32[4]{0:T(128)S(1)} %pad_add_fusion.meta, f32[5,4,448,256]{3,2,1,0:T(8,128)} %state.3), custom_call_target="tpu_custom_call" | custom-call | tf_op jit(solution)/shard_map/edges/pallas_call | solution.py:539
  5.8 0.1 collective-permute-start
  5.8 0.6 collective-permute-start.1
  6.4 1.5 %collective-permute-start.2 = (f32[24,448]{1,0:T(8,128)S(1)}, f32[24,448]{1,0:T(8,128)S(1)}, u32[]{:S(2)}, u32[]{:S(2)}) collective-permute-start(f32[24,448]{1,0:T(8,128)S(1)} %get-tuple-element.29), channel_id=1, source_target_pairs={{0,8},{8,0},{16,24},{24,16},{1,9},{9,1},{17,25},{25,17},{2,10},{10... | collective-permute-start | bytes 129032 | tf_op jit(solution)/shard_map/halo/ppermute | solution.py:559
  7.9 2.0 %collective-permute-start.3 = (f32[24,448]{1,0:T(8,128)S(1)}, f32[24,448]{1,0:T(8,128)S(1)}, u32[]{:S(2)}, u32[]{:S(2)}) collective-permute-start(f32[24,448]{1,0:T(8,128)S(1)} %get-tuple-element.30), channel_id=1, source_target_pairs={{8,16},{16,8},{9,17},{17,9},{10,18},{18,10},{11,19},{19,11},{12,20... | collective-permute-start | bytes 129032 | tf_op jit(solution)/shard_map/halo/ppermute | solution.py:560
  9.9 0.2 fusion.4
  10.1 0.1 copy.24.strips
  10.2 0.1 reshape.14.coupling
  10.3 0.5 collective-permute-done.2.lat_pair
  10.8 4.5 %collective-permute-done.3.lat_cross = f32[24,448]{1,0:T(8,128)S(1)} collective-permute-done((f32[24,448]{1,0:T(8,128)S(1)}, f32[24,448]{1,0:T(8,128)S(1)}, u32[]{:S(2)}, u32[]{:S(2)}) %collective-permute-start.3) | collective-permute-done | bytes 43040 | tf_op jit(solution)/shard_map/halo/ppermute | solution.py:560
  15.2 13.6 %stencil.1 = (f32[5,4,448,256]{3,2,1,0:T(8,128)}, f32[448,128]{1,0:T(8,128)S(1)}, f32[448,128]{1,0:T(8,128)S(1)}, f32[16,256]{1,0:T(8,128)S(1)}, f32[296,256]{1,...) custom-call(s32[4]{0:T(128)S(1)} %pad_add_fusion.meta, ...), custom_call_target="tpu_custom_call" | custom-call | tf_op jit(solution)/shard_map/stencil/pallas_call | solution.py:565
  28.8 0.1 collective-permute-start.4
  29.0 0.1 fusion.10
  29.1 0.1 copy.25.begins
  29.2 2.1 %collective-permute-start.9 = (f32[96,256]{1,0:T(8,128)S(1)}, f32[96,256]{1,0:T(8,128)S(1)}, u32[]{:S(2)}, u32[]{:S(2)}) collective-permute-start(f32[96,256]{1,0:T(8,128)S(1)} %get-tuple-element.44), channel_id=1, source_target_pairs={{1,4},{4,1},{3,6},{6,3},{5,0},{0,5},{7,2},{2,7},{9,12},{12,9},{11,... | collective-permute-start | bytes 294920 | tf_op jit(solution)/shard_map/exchange/ppermute | solution.py:599
  31.3 0.8 %collective-permute-start.10 = (f32[96,256]{1,0:T(8,128)S(1)}, f32[96,256]{1,0:T(8,128)S(1)}, u32[]{:S(2)}, u32[]{:S(2)}) collective-permute-start(f32[96,256]{1,0:T(8,128)S(1)} %get-tuple-element.45), channel_id=1, source_target_pairs={{0,4},{4,0},{1,5},{5,1},{2,6},{6,2},{3,7},{7,3},{8,12},{12,8},{9,1... | collective-permute-start | bytes 294920 | tf_op jit(solution)/shard_map/exchange/ppermute | solution.py:599
  32.1 3.1 %collective-permute-start.6 = (f32[112,256]{1,0:T(8,128)S(1)}, f32[112,256]{1,0:T(8,128)S(1)}, u32[]{:S(2)}, u32[]{:S(2)}) collective-permute-start(f32[112,256]{1,0:T(8,128)S(1)} %get-tuple-element.39), channel_id=1, source_target_pairs={{0,2},{2,0},{1,3},{3,1},{4,6},{6,4},{5,7},{7,5},{8,10},{10,8},{9,1... | collective-permute-start | bytes 344072 | tf_op jit(solution)/shard_map/exchange/ppermute | solution.py:599
  35.3 0.0 collective-permute-start.5
  35.3 0.6 %near.8 = (f32[6,448,128]{2,1,0:T(8,128)S(1)}, f32[6,32,256]{2,1,0:T(8,128)S(1)}, f32[112,256]{1,0:T(8,128)S(1)}) custom-call(s32[4]{0:T(128)S(1)} %pad_add_fusion.meta, f32[448,128]{1,0:T(8,128)S(1)} %get-tuple-element.31.cosine, f32[448,128]{1,0:T(8,128)S(1)} %get-tuple-element.32.sine, ...), custom_call_target="tpu_custom_call", output_to_operand_aliasing={{2}: (6, {})} | custom-call | flops 1849688064 | bytes 2752512 | tf_op jit(solution)/shard_map/near/pallas_call | solution.py:609
  35.9 0.0 collective-permute-done.4.rest_1_
  35.9 1.1 %collective-permute-start.7 = (f32[112,256]{1,0:T(8,128)S(1)}, f32[112,256]{1,0:T(8,128)S(1)}, u32[]{:S(2)}, u32[]{:S(2)}) collective-permute-start(f32[112,256]{1,0:T(8,128)S(1)} %get-tuple-element.42), channel_id=1, source_target_pairs={{2,4},{4,2},{3,5},{5,3},{6,0},{0,6},{7,1},{1,7},{10,12},{12,10},{1... | collective-permute-start | bytes 344072 | tf_op jit(solution)/shard_map/late_exchange/ppermute | solution.py:599
  37.1 0.6 %near.6 = (f32[6,448,128]{2,1,0:T(8,128)S(1)}, f32[6,32,256]{2,1,0:T(8,128)S(1)}, f32[96,256]{1,0:T(8,128)S(1)}, f32[296,256]{1,0:T(8,128)S(1)}) custom-call(s32[4]{0:T(128)S(1)} %pad_add_fusion.meta, f32[448,128]{1,0:T(8,128)S(1)} %get-tuple-element.31.cosine, f32[448,128]{1,0:T(8,128)S(1)} %get-tuple-element.32.sine, ...), custom_call_target="tpu_custom_call", output_to_operand_aliasing={{2}: (6, {}), {3}: (7, {})} | custom-call | flops 1849688064 | bytes 2752512 | tf_op jit(solution)/shard_map/near/pallas_call | solution.py:609
  37.7 7.4 %collective-permute-done.6.rest_0_ = f32[112,256]{1,0:T(8,128)S(1)} collective-permute-done((f32[112,256]{1,0:T(8,128)S(1)}, f32[112,256]{1,0:T(8,128)S(1)}, u32[]{:S(2)}, u32[]{:S(2)}) %collective-permute-start.6) | collective-permute-done | bytes 114720 | tf_op jit(solution)/shard_map/exchange/ppermute | solution.py:599
  45.1 0.0 collective-permute-start.8
  45.1 0.6 %near.7 = (f32[8,448,128]{2,1,0:T(8,128)S(1)}, f32[8,32,256]{2,1,0:T(8,128)S(1)}, f32[112,256]{1,0:T(8,128)S(1)}) custom-call(s32[4]{0:T(128)S(1)} %pad_add_fusion.meta, f32[448,128]{1,0:T(8,128)S(1)} %get-tuple-element.31.cosine, f32[448,128]{1,0:T(8,128)S(1)} %get-tuple-element.32.sine, ...), custom_call_target="tpu_custom_call", output_to_operand_aliasing={{2}: (6, {})} | custom-call | flops 2466250752 | bytes 3670016 | tf_op jit(solution)/shard_map/near/pallas_call | solution.py:609
  45.7 0.0 collective-permute-done.9.rest_5_
  45.7 0.0 collective-permute-done.10.rest_6_
  45.7 9.3 %collective-permute-done.7.rest_3_ = f32[112,256]{1,0:T(8,128)S(1)} collective-permute-done((f32[112,256]{1,0:T(8,128)S(1)}, f32[112,256]{1,0:T(8,128)S(1)}, u32[]{:S(2)}, u32[]{:S(2)}) %collective-permute-start.7) | collective-permute-done | bytes 114720 | tf_op jit(solution)/shard_map/late_exchange/ppermute | solution.py:599
  55.1 2.0 %far.2 = (f32[5,4,448,256]{3,2,1,0:T(8,128)}, f32[1,5,4,2048]{3,2,1,0:T(4,128)}) custom-call(s32[4]{0:T(128)S(1)} %pad_add_fusion.meta, s32[8,2]{1,0:T(8,128)S(1)} %copy.25.begins, f32[448,128]{1,0:T(8,128)S(1)} %get-tuple-element.31.cosine, f32[448,128]{1,0:T(8,128)S(1)} %get-tuple-element.32.sine, ...), custom_call_target="tpu_custom_call", output_to_operand_aliasing={{0}: (21, {})} | custom-call | tf_op jit(solution)/shard_map/far/pallas_call | solution.py:645
  (29 shorter events, 0.1 us)
Async XLA Ops:
  0.6 9.3 %copy-start.9 = (s32[44]{0:T(128)S(1)}, s32[44]{0:T(128)}, u32[]{:S(2)}) copy-start(s32[44]{0:T(128)} %constant.71.clone) | copy-start | bytes 532
  0.6 14.6 %copy-start.2 = (bf16[144,448]{1,0:T(8,128)(2,1)S(1)}, bf16[144,448]{1,0:T(8,128)(2,1)}, u32[]{:S(2)}) copy-start(bf16[144,448]{1,0:T(8,128)(2,1)} %constant.69.clone.send) | copy-start | bytes 387076
  0.7 9.2 %copy-start.8 = (s32[256]{0:T(256)S(1)}, s32[256]{0:T(256)}, u32[]{:S(2)}) copy-start(s32[256]{0:T(256)} %param.16) | copy-start | bytes 3076
  0.7 9.4 %copy-start.6 = (s32[8,4]{0,1:T(4,128)S(1)}, s32[8,4]{0,1:T(4,128)}, u32[]{:S(2)}) copy-start(s32[8,4]{0,1:T(4,128)} %param.17) | copy-start | bytes 388
  0.7 9.5 %copy-start.5 = (f32[4,5,5]{2,0,1:T(4,128)S(1)}, f32[4,5,5]{2,0,1:T(4,128)}, u32[]{:S(2)}) copy-start(f32[4,5,5]{2,0,1:T(4,128)} %param.15) | copy-start | bytes 1204
  0.7 14.6 %copy-start.4 = (f32[2,256]{1,0:T(2,128)S(1)}, f32[2,256]{1,0:T(2,128)}, u32[]{:S(2)}) copy-start(f32[2,256]{1,0:T(2,128)} %diffusion.1) | copy-start | bytes 6148
  0.8 28.2 %copy-start.10 = (f32[7]{0:T(128)S(1)}, f32[7]{0:T(128)}, u32[]{:S(2)}) copy-start(f32[7]{0:T(128)} %constant.79) | copy-start | bytes 88
  0.8 28.2 %copy-start.11 = (s32[7]{0:T(128)S(1)}, s32[7]{0:T(128)}, u32[]{:S(2)}) copy-start(s32[7]{0:T(128)} %constant.72.clone) | copy-start | bytes 88
  0.8 28.3 %copy-start.7 = (s32[1,8,2]{1,2,0:T(2,128)S(1)}, s32[1,8,2]{1,2,0:T(2,128)}, u32[]{:S(2)}) copy-start(s32[1,8,2]{1,2,0:T(2,128)} %param.18) | copy-start | bytes 196
  0.8 34.5 %copy-start = (bf16[960,224]{1,0:T(8,128)(2,1)S(1)}, bf16[960,224]{1,0:T(8,128)(2,1)}, u32[]{:S(2)}) copy-start(bf16[960,224]{1,0:T(8,128)(2,1)} %constant.68.clone.near) | copy-start | bytes 1290244
  5.8 4.5 %collective-permute-start = (f32[24,256]{1,0:T(8,128)S(1)}, f32[24,256]{1,0:T(8,128)S(1)}, u32[]{:S(2)}, u32[]{:S(2)}) collective-permute-start(f32[24,256]{1,0:T(8,128)S(1)} %get-tuple-element.27), channel_id=1, source_target_pairs={{0,1},{1,0},{2,3},{3,2},{4,5},{5,4},{6,7},{7,6},{8,9},{9,8},{10,11... | collective-permute-start | bytes 73736 | tf_op jit(solution)/shard_map/halo/ppermute | solution.py:557
  5.8 4.4 %collective-permute-start.1 = (f32[24,256]{1,0:T(8,128)S(1)}, f32[24,256]{1,0:T(8,128)S(1)}, u32[]{:S(2)}, u32[]{:S(2)}) collective-permute-start(f32[24,256]{1,0:T(8,128)S(1)} %get-tuple-element.28), channel_id=1, source_target_pairs={{1,2},{2,1},{3,4},{4,3},{5,6},{6,5},{7,0},{0,7},{9,10},{10,9},{11,... | collective-permute-start | bytes 73736 | tf_op jit(solution)/shard_map/halo/ppermute | solution.py:558
  6.4 4.4 %collective-permute-start.2 = (f32[24,448]{1,0:T(8,128)S(1)}, f32[24,448]{1,0:T(8,128)S(1)}, u32[]{:S(2)}, u32[]{:S(2)}) collective-permute-start(f32[24,448]{1,0:T(8,128)S(1)} %get-tuple-element.29), channel_id=1, source_target_pairs={{0,8},{8,0},{16,24},{24,16},{1,9},{9,1},{17,25},{25,17},{2,10},{10... | collective-permute-start | bytes 129032 | tf_op jit(solution)/shard_map/halo/ppermute | solution.py:559
  7.9 7.4 %collective-permute-start.3 = (f32[24,448]{1,0:T(8,128)S(1)}, f32[24,448]{1,0:T(8,128)S(1)}, u32[]{:S(2)}, u32[]{:S(2)}) collective-permute-start(f32[24,448]{1,0:T(8,128)S(1)} %get-tuple-element.30), channel_id=1, source_target_pairs={{8,16},{16,8},{9,17},{17,9},{10,18},{18,10},{11,19},{19,11},{12,20... | collective-permute-start | bytes 129032 | tf_op jit(solution)/shard_map/halo/ppermute | solution.py:560
  28.8 7.1 %collective-permute-start.4 = (f32[296,256]{1,0:T(8,128)S(1)}, f32[296,256]{1,0:T(8,128)S(1)}, u32[]{:S(2)}, u32[]{:S(2)}) collective-permute-start(f32[296,256]{1,0:T(8,128)S(1)} %get-tuple-element.36), channel_id=1, source_target_pairs={{0,1},{1,0},{2,3},{3,2},{4,5},{5,4},{6,7},{7,6},{8,9},{9,8},{10,11... | collective-permute-start | bytes 909320 | tf_op jit(solution)/shard_map/exchange/ppermute | solution.py:599
  29.2 16.5 %collective-permute-start.9 = (f32[96,256]{1,0:T(8,128)S(1)}, f32[96,256]{1,0:T(8,128)S(1)}, u32[]{:S(2)}, u32[]{:S(2)}) collective-permute-start(f32[96,256]{1,0:T(8,128)S(1)} %get-tuple-element.44), channel_id=1, source_target_pairs={{1,4},{4,1},{3,6},{6,3},{5,0},{0,5},{7,2},{2,7},{9,12},{12,9},{11,... | collective-permute-start | bytes 294920 | tf_op jit(solution)/shard_map/exchange/ppermute | solution.py:599
  31.3 14.4 %collective-permute-start.10 = (f32[96,256]{1,0:T(8,128)S(1)}, f32[96,256]{1,0:T(8,128)S(1)}, u32[]{:S(2)}, u32[]{:S(2)}) collective-permute-start(f32[96,256]{1,0:T(8,128)S(1)} %get-tuple-element.45), channel_id=1, source_target_pairs={{0,4},{4,0},{1,5},{5,1},{2,6},{6,2},{3,7},{7,3},{8,12},{12,8},{9,1... | collective-permute-start | bytes 294920 | tf_op jit(solution)/shard_map/exchange/ppermute | solution.py:599
  32.1 12.9 %collective-permute-start.6 = (f32[112,256]{1,0:T(8,128)S(1)}, f32[112,256]{1,0:T(8,128)S(1)}, u32[]{:S(2)}, u32[]{:S(2)}) collective-permute-start(f32[112,256]{1,0:T(8,128)S(1)} %get-tuple-element.39), channel_id=1, source_target_pairs={{0,2},{2,0},{1,3},{3,1},{4,6},{6,4},{5,7},{7,5},{8,10},{10,8},{9,1... | collective-permute-start | bytes 344072 | tf_op jit(solution)/shard_map/exchange/ppermute | solution.py:599
  35.3 19.8 %collective-permute-start.5 = (f32[296,256]{1,0:T(8,128)S(1)}, f32[296,256]{1,0:T(8,128)S(1)}, u32[]{:S(2)}, u32[]{:S(2)}) collective-permute-start(f32[296,256]{1,0:T(8,128)S(1)} %get-tuple-element.38), channel_id=1, source_target_pairs={{1,2},{2,1},{3,4},{4,3},{5,6},{6,5},{7,0},{0,7},{9,10},{10,9},{11,... | collective-permute-start | bytes 909320 | tf_op jit(solution)/shard_map/exchange/ppermute | solution.py:599
  35.9 19.1 %collective-permute-start.7 = (f32[112,256]{1,0:T(8,128)S(1)}, f32[112,256]{1,0:T(8,128)S(1)}, u32[]{:S(2)}, u32[]{:S(2)}) collective-permute-start(f32[112,256]{1,0:T(8,128)S(1)} %get-tuple-element.42), channel_id=1, source_target_pairs={{2,4},{4,2},{3,5},{5,3},{6,0},{0,6},{7,1},{1,7},{10,12},{12,10},{1... | collective-permute-start | bytes 344072 | tf_op jit(solution)/shard_map/late_exchange/ppermute | solution.py:599
  37.1 18.0 %copy-start.1 = (bf16[448,240]{1,0:T(8,128)(2,1)S(1)}, bf16[448,240]{1,0:T(8,128)(2,1)}, u32[]{:S(2)}) copy-start(bf16[448,240]{1,0:T(8,128)(2,1)} %constant.70.clone.far) | copy-start | bytes 645124
  37.1 18.0 %copy-start.3 = (bf16[128,512]{1,0:T(8,128)(2,1)S(1)}, bf16[128,512]{1,0:T(8,128)(2,1)}, u32[]{:S(2)}) copy-start(bf16[128,512]{1,0:T(8,128)(2,1)} %constant.74.clone.hats) | copy-start | bytes 393220
  45.1 10.0 %collective-permute-start.8 = (f32[96,256]{1,0:T(8,128)S(1)}, f32[96,256]{1,0:T(8,128)S(1)}, u32[]{:S(2)}, u32[]{:S(2)}) collective-permute-start(f32[96,256]{1,0:T(8,128)S(1)} %get-tuple-element.43), channel_id=1, source_target_pairs={{0,3},{3,0},{2,5},{5,2},{4,7},{7,4},{6,1},{1,6},{8,11},{11,8},{10,... | collective-permute-start | bytes 294920 | tf_op jit(solution)/shard_map/late_exchange/ppermute | solution.py:599
